TPU v7x, 32 devices: a whole 2x2x4 slice. The times are simulated.
32 devices in a mesh: row: 2 (over x), col: 16 (over z, y, core).
Axes of the slice: x: 2, y: 2, z: 4, core: 2. Of those that a mesh axis runs over, the one named last changes fastest.
Arguments:
- left_features: bfloat16 [8, 1024, 320], P('row', 'col'), may hold values from -6 to 6
- right_features: bfloat16 [8, 1024, 320], P('row', 'col'), may hold values from -6 to 6
- conv_weight: bfloat16 [3, 3, 3, 40, 32], replicated, may hold values from -0.1875 to 0.1875
- cotangent: bfloat16 [24, 8, 1024, 32], P(None, 'row', 'col'), may hold values from -6 to 6
Outputs:
- cost_output: bfloat16 [24, 8, 1024, 32], P(None, 'row', 'col')
- weight_grad: float32 [3, 3, 3, 40, 32], replicated
- left_grad: bfloat16 [8, 1024, 320], P('row', 'col')
- right_grad: bfloat16 [8, 1024, 320], P('row', 'col')
All inputs are finite; a program needn't handle non-finite values.
Results may differ from a plain program's by a relative error of at most 0.0049.
Values may be sent and summed in bfloat16 or wider, within the bound.
No kernel may reach another device: no remote copies, remote signals or barrier semaphores. Data moves between devices by JAX's collectives and lax.ppermute only.
A program may use at most 128 MiB of HBM per device.

v0:
```python
import math

import jax
import jax.numpy as jnp
from jax import lax
from jax.sharding import PartitionSpec as P

DISP = 24
STEP = 4


DIMS = ("NDHWC", "DHWIO", "NDHWC")
KERNEL_DIMS = ("CDHWN", "IDHWO", "NDHWC")


def shifted_2(block, axis, distance):
    devices = range(lax.axis_size(axis))
    route = [(i - distance, i) for i in devices if i - distance in devices]
    return lax.ppermute(block, axis, route)


def with_halo(cells, sides, width):
    for axis, dim in sides:
        count = lax.axis_size(axis)
        ends = count - 1
        head = lax.slice_in_dim(cells, 0, width, axis=dim)
        tail = lax.slice_in_dim(cells, cells.shape[dim] - width, cells.shape[dim], axis=dim)
        cells = jnp.concatenate(
            [
                lax.ppermute(tail, axis, [(i, (i + 1) % count) for i in range(ends)]),
                cells,
                lax.ppermute(head, axis, [((i + 1) % count, i) for i in range(ends)]),
            ],
            axis=dim,
        )
    return cells


def conv_valid(padded_input, kernel):
    return lax.conv_general_dilated(
        padded_input[None],
        kernel,
        (1, 1, 1),
        ((1, 1), (0, 0), (0, 0)),
        dimension_numbers=DIMS,
        preferred_element_type=jnp.float32,
    )[0]


def on_device(left_features, right_features, conv_weight, cotangent):
    tile_rows, tile_cols, channels = left_features.shape
    groups = conv_weight.shape[3]
    group_size = channels // groups
    reach_cols = STEP * (DISP - 1)
    hop_count = -(-reach_cols // tile_cols)
    band_base = hop_count * tile_cols
    band_width = band_base + tile_cols
    pieces = [right_features]
    carried = right_features
    for hop_index in range(hop_count):
        carried = shifted_2(carried, "col", 1)
        pieces.insert(0, carried)
    right_band = jnp.concatenate(pieces, axis=1)
    group_table = (
        jnp.arange(channels)[:, None] // group_size == jnp.arange(groups)[None, :]
    ).astype(jnp.float32)
    left_float = left_features.astype(jnp.float32)
    planes = []
    for disp_index in range(DISP):
        band_start = band_base - STEP * disp_index
        shifted = right_band[:, band_start : band_start + tile_cols].astype(jnp.float32)
        planes.append(
            jnp.einsum(
                "hwc,cg->hwg", left_float * shifted, group_table, precision=lax.Precision.HIGHEST
            )
        )
    volume = (jnp.stack(planes) / group_size).astype(jnp.bfloat16)
    padded_volume = with_halo(volume, (("row", 1), ("col", 2)), 1)
    output = conv_valid(padded_volume, conv_weight).astype(jnp.bfloat16)
    padded_cotangent = with_halo(cotangent, (("row", 1), ("col", 2)), 1)
    flipped = jnp.transpose(conv_weight[::-1, ::-1, ::-1], (0, 1, 2, 4, 3))
    grad_volume = conv_valid(padded_cotangent, flipped).astype(jnp.bfloat16)
    full_pad = jnp.pad(padded_volume, ((1, 1), (0, 0), (0, 0), (0, 0)))
    kernel_raw = lax.conv_general_dilated(
        full_pad[None],
        cotangent[None],
        (1, 1, 1),
        ((0, 0), (0, 0), (0, 0)),
        dimension_numbers=KERNEL_DIMS,
        preferred_element_type=jnp.float32,
    )
    local_grad = jnp.transpose(kernel_raw, (1, 2, 3, 0, 4))
    total_cells = DISP * tile_rows * lax.axis_size("row") * tile_cols * lax.axis_size("col")
    weight_grad = lax.psum(local_grad, ("row", "col")) / math.sqrt(total_cells)
    left_accum = jnp.zeros((tile_rows, tile_cols, channels), jnp.float32)
    grad_band = jnp.zeros((tile_rows, band_width, channels), jnp.float32)
    for disp_index in range(DISP):
        band_start = band_base - STEP * disp_index
        shifted = right_band[:, band_start : band_start + tile_cols].astype(jnp.float32)
        spread = jnp.einsum(
            "hwg,cg->hwc",
            grad_volume[disp_index].astype(jnp.float32),
            group_table,
            precision=lax.Precision.HIGHEST,
        )
        left_accum = left_accum + spread * shifted
        contrib = spread * left_float
        grad_band = grad_band + jnp.pad(
            contrib, ((0, 0), (band_start, band_width - band_start - tile_cols), (0, 0))
        )

    def band_piece(hop_index):
        return grad_band[
            :, band_base - hop_index * tile_cols : band_base - (hop_index - 1) * tile_cols
        ]

    right_accum = band_piece(hop_count)
    for hop_index in range(hop_count - 1, -1, -1):
        right_accum = shifted_2(right_accum, "col", -1) + band_piece(hop_index)
    left_grad = (left_accum / group_size).astype(jnp.bfloat16)
    right_grad = (right_accum / group_size).astype(jnp.bfloat16)
    return (output, weight_grad, left_grad, right_grad)


def solution(mesh):
    in_specs = (P("row", "col", None), P("row", "col", None), P(), P(None, "row", "col", None))
    out_specs = (P(None, "row", "col", None), P(), P("row", "col", None), P("row", "col", None))
    return jax.shard_map(
        on_device, mesh=mesh, in_specs=in_specs, out_specs=out_specs, check_vma=False
    )
```

profile of v0, /device:TPU:0, one launch (start us, length us, event | category | flops | bytes accessed | tf_op | source)
XLA Modules:
  0.0 355.3 jit_solution(13402125338160111373)
XLA Ops:
  7.2 2.0 copy.212
  9.3 5.0 %collective-permute-start.6 = (bf16[24,1,64,32]{3,0,2,1:T(8,128)(2,1)S(1)}, bf16[24,1,64,32]{3,0,2,1:T(8,128)(2,1)S(1)}, u32[]{:S(2)}, u32[]{:S(2)}) collective-permute-start(bf16[24,1,64,32]{3,0,2,1:T(8,128)(2,1)S(1)} %get-tuple-element.46), channel_id=1, source_target_pairs={{0,16},{1,17},{2,18},{3,19},{4,20},{5,21},{6,22},{7,23},{8,24},{9,... | collective-permute-start | bytes 294920 | tf_op jit(solution)/shard_map/ppermute | solution.py:30
  14.3 1.3 collective-permute-start.7
  15.6 2.2 collective-permute-start
  17.8 4.9 %collective-permute-done.6 = bf16[24,1,64,32]{3,0,2,1:T(8,128)(2,1)S(1)} collective-permute-done((bf16[24,1,64,32]{3,0,2,1:T(8,128)(2,1)S(1)}, bf16[24,1,64,32]{3,0,2,1:T(8,128)(2,1)S(1)}, u32[]{:S(2)}, u32[]{:S(2)}) %collective-permute-start.6) | collective-permute-done | bytes 98336 | tf_op jit(solution)/shard_map/ppermute | solution.py:30
  22.7 4.1 %collective-permute-done.7 = bf16[24,1,64,32]{3,0,2,1:T(8,128)(2,1)S(1)} collective-permute-done((bf16[24,1,64,32]{3,0,2,1:T(8,128)(2,1)S(1)}, bf16[24,1,64,32]{3,0,2,1:T(8,128)(2,1)S(1)}, u32[]{:S(2)}, u32[]{:S(2)}) %collective-permute-start.7) | collective-permute-done | bytes 98336 | tf_op jit(solution)/shard_map/ppermute | solution.py:32
  27.6 1.3 collective-permute-start.8
  28.9 1.3 collective-permute-start.9
  30.2 1.1 fusion.45
  31.3 5.1 %copy.211 = bf16[1,24,4,64,32]{4,0,3,2,1:T(2,128)(2,1)} copy(bf16[1,24,4,64,32]{3,4,2,1,0:T(8,128)(2,1)S(1)} %bitcast.279) | data formatting | bytes 786432 | tf_op jit(solution)/shard_map/broadcast_in_dim | solution.py:86
  36.4 2.5 maximum_bitcast_fusion
  40.1 5.4 %select_convert_fusion = bf16[24,4,8,9,40]{4,2,3,1,0:T(8,128)(2,1)S(1)} fusion(pred[8,9]{0,1:T(8,128)(4,1)S(1)} %copy-done.29, bf16[3,3,3,40,32]{3,4,2,1,0:T(8,128)(2,1)S(1)} %copy-done, bf16[24,6,1,7,2,32]{5,3,4,1,0,2:T(8,128)(2,1)S(1)} %slice.377, bf16[24,6,1,8,9,32]{5,3,4,1,0,2:T(8,128)(2,1)S(1)} %copy.216), kind=kOutput, calls=%fused_computation.52 | convolution fusion | flops 467472384 | bytes 1414728 | tf_op jit(solution)/shard_map/conv_general_dilated | solution.py:40
  49.7 1.0 copy.239
  51.3 0.9 copy.277
  52.2 1.0 fusion.118
  54.8 0.9 copy.276
  55.7 1.0 fusion.120
  59.2 1.0 fusion.122
  61.8 0.9 copy.274
  62.8 1.0 fusion.124
  66.3 1.1 fusion.126
  69.9 1.0 fusion.128
  73.4 1.0 fusion.130
  76.0 0.9 copy.270
  76.9 1.0 fusion.132
  80.4 1.0 fusion.134
  83.9 1.0 fusion.136
  86.5 0.9 copy.267
  87.4 1.0 fusion.138
  90.0 0.9 copy.266
  91.1 1.0 fusion.100
  92.3 1.0 fusion.102
  93.4 1.0 fusion.104
  95.0 6.1 %convert_multiply_fusion.23 = (f32[4,64,320]{2,1,0:T(8,128)}, f32[4,64,320]{2,1,0:T(8,128)}, f32[4,64,320]{2,1,0:T(8,128)}, f32[4,64,320]{2,1,0:T(8,128)}, f32[4...) fusion(bf16[4,64,320]{2,1,0:T(8,128)(2,1)S(1)} %copy-done.1, ...), kind=kOutput, calls=%fused_computation.27 | convolution fusion | flops 8122880 | bytes 11982080 | tf_op jit(solution)/shard_map/hwg,cg->hwc/dot_general | solution.py:100
  101.4 5.3 %collective-permute-start.1 = (bf16[4,64,320]{2,1,0:T(8,128)(2,1)}, bf16[4,64,320]{2,1,0:T(8,128)(2,1)S(1)}, u32[]{:S(2)}, u32[]{:S(2)}) collective-permute-start(bf16[4,64,320]{2,1,0:T(8,128)(2,1)} %collective-permute-done), channel_id=1, source_target_pairs={{0,1},{1,2},{2,3},{3,4},{4,5},{5,6},{6,7},{7,8},{8,9},{9,10},{10,1... | collective-permute-start | bytes 491528 | tf_op jit(solution)/shard_map/ppermute | solution.py:19
  107.6 1.0 constant_dynamic-update-slice_fusion.2
  116.4 1.4 fusion.29
  121.8 1.7 collective-permute-start.2
  123.6 1.3 collective-permute-start.3
  125.0 3.0 multiply_convert_fusion.1
  128.1 1.5 convert_multiply_fusion.5
  129.5 2.4 collective-permute-done.3
  132.3 1.8 fusion.250
  134.1 2.3 copy.202
  136.4 4.2 %collective-permute-start.4 = (bf16[24,6,1,40]{3,0,2,1:T(8,128)(2,1)S(1)}, bf16[24,6,1,40]{3,0,2,1:T(8,128)(2,1)S(1)}, u32[]{:S(2)}, u32[]{:S(2)}) collective-permute-start(bf16[24,6,1,40]{3,0,2,1:T(8,128)(2,1)S(1)} %copy.202), channel_id=1, source_target_pairs={{0,1},{1,2},{2,3},{3,4},{4,5},{5,6},{6,7},{7,8},{8,9},{9,10},{10,1... | collective-permute-start | bytes 34568 | tf_op jit(solution)/shard_map/ppermute | solution.py:30
  140.6 0.9 copy.203
  141.6 1.3 collective-permute-start.5
  142.9 4.3 %pad_add_fusion = f32[4,192,320]{2,1,0:T(8,128)S(1)} fusion(f32[4,64,320]{2,1,0:T(8,128)} %get-tuple-element.75, f32[4,64,320]{2,1,0:T(8,128)} %get-tuple-element.74, f32[4,64,320]{2,1,0:T(8,128)} %get-tuple-element.73, f32[4,64,320]{2,1,0:T(8,128)} %get-tuple-element.72, f32[4,64,320]{2,1,0:T(8,128)} %get-tuple-element.71, ...), kind=kLoop, calls=%fused_computation.74 | loop fusion | flops 5652480 | bytes 8847360 | tf_op jit(solution)/shard_map/add | solution.py:108
  148.0 1.3 collective-permute-start.10
  149.3 1.0 copy.204
  150.3 2.1 copy.205
  152.4 2.7 pad_maximum_fusion.1
  155.1 1.5 pad_bitcast_fusion
  156.7 12.4 %copy.210 = bf16[1,26,6,66,40]{4,0,3,2,1:T(2,128)(2,1)} copy(bf16[1,26,6,66,40]{3,4,2,1,0:T(8,128)(2,1)} %pad_bitcast_fusion) | data formatting | bytes 1647360 | tf_op jit(solution)/shard_map/broadcast_in_dim | solution.py:85
  169.0 42.7 %fusion.252 = f32[3,3,3,40,32]{3,4,2,1,0:T(8,128)} fusion(bf16[1,26,6,66,40]{4,0,3,2,1:T(2,128)(2,1)} %copy.210, bf16[1,24,4,64,32]{4,0,3,2,1:T(2,128)(2,1)} %copy.211), kind=kOutput, calls=%fused_computation.321 | convolution fusion | flops 424673280 | bytes 1355136 | tf_op jit(solution)/shard_map/transpose | solution.py:92
  211.8 3.9 %fusion.257 = bf16[24,6,1,66,40]{3,4,1,0,2:T(8,128)(2,1)} fusion(bf16[24,6,1,40]{2,3,1,0:T(8,128)(2,1)} %copy.205, bf16[24,1,64,40]{2,3,1,0:T(8,128)(2,1)S(1)} %collective-permute-done.3, bf16[24,4,64,40]{2,3,1,0:T(8,128)(2,1)S(1)} %multiply_convert_fusion, bf16[24,1,64,40]{2,3,1,0:T(8,128)(2,1)S(1)} %collective-permute-done.2, ...), kind=kLoop, calls=%fused_computation.322 | loop fusion | flops 3801600 | bytes 1520640 | tf_op jit(solution)/shard_map/broadcast_in_dim | solution.py:41
  215.6 3.3 copy.290
  219.9 6.0 %select_convert_fusion.1 = bf16[24,4,8,9,32]{4,2,3,1,0:T(8,128)(2,1)S(1)} fusion(pred[8,9]{0,1:T(8,128)(4,1)S(1)} %copy-done.29, bf16[3,3,3,40,32]{3,4,2,1,0:T(8,128)(2,1)S(1)} %copy-done, bf16[24,6,1,7,2,40]{5,3,4,1,0,2:T(8,128)(2,1)S(1)} %slice.373, bf16[24,6,1,8,9,40]{5,3,4,1,0,2:T(8,128)(2,1)S(1)} %copy.208), kind=kOutput, calls=%fused_computation.53 | convolution fusion | flops 467970048 | bytes 1502280 | tf_op jit(solution)/shard_map/conv_general_dilated | solution.py:40
  227.2 1.8 slice_add_fusion.1
  229.0 1.3 collective-permute-start.11
  230.6 1.7 copy.265
  232.3 112.4 %all-reduce.27.cloned.1.call-done = f32[3,3,3,40,32]{3,4,2,1,0:T(8,128)} async-done(((f32[3,3,3,40,32]{3,4,2,1,0:T(8,128)}), f32[3,3,3,40,32]{3,4,2,1,0:T(8,128)}) %all-reduce.27.cloned.1.call-update) | async-done | bytes 138256 | tf_op jit(solution)/shard_map/psum | solution.py:94
  344.7 1.8 broadcast_multiply_fusion
  346.5 1.8 fusion.70
  (185 shorter events, 46.7 us)
Async XLA Ops:
  7.2 32.8 %copy-start = (bf16[3,3,3,40,32]{3,4,2,1,0:T(8,128)(2,1)S(1)}, bf16[3,3,3,40,32]{3,4,2,1,0:T(8,128)(2,1)}, u32[]{:S(2)}) copy-start(bf16[3,3,3,40,32]{3,4,2,1,0:T(8,128)(2,1)} %param.6) | copy-start | bytes 207364
  7.2 8.5 %copy-start.27 = (bf16[4,64,320]{2,1,0:T(8,128)(2,1)S(1)}, bf16[4,64,320]{2,1,0:T(8,128)(2,1)}, u32[]{:S(2)}) copy-start(bf16[4,64,320]{2,1,0:T(8,128)(2,1)} %param.5) | copy-start | bytes 491524
  7.2 337.5 %all-reduce.27.cloned.1.call-start = ((), (), s32[]{:S(2)}) async-start(), calls=%async_computation | async-start | bytes 884736 | tf_op jit(solution)/shard_map/psum | solution.py:94
  9.2 21.0 %copy-start.1 = (bf16[4,64,320]{2,1,0:T(8,128)(2,1)S(1)}, bf16[4,64,320]{2,1,0:T(8,128)(2,1)}, u32[]{:S(2)}) copy-start(bf16[4,64,320]{2,1,0:T(8,128)(2,1)} %param.4) | copy-start | bytes 491524
  9.2 22.1 %copy-start.4 = (bf16[24,4,64,32]{2,3,1,0:T(8,128)(2,1)S(1)}, bf16[24,4,64,32]{2,3,1,0:T(8,128)(2,1)}, u32[]{:S(2)}) copy-start(bf16[24,4,64,32]{2,3,1,0:T(8,128)(2,1)} %param.7) | copy-start | bytes 1179652
  9.3 13.3 %collective-permute-start.6 = (bf16[24,1,64,32]{3,0,2,1:T(8,128)(2,1)S(1)}, bf16[24,1,64,32]{3,0,2,1:T(8,128)(2,1)S(1)}, u32[]{:S(2)}, u32[]{:S(2)}) collective-permute-start(bf16[24,1,64,32]{3,0,2,1:T(8,128)(2,1)S(1)} %get-tuple-element.46), channel_id=1, source_target_pairs={{0,16},{1,17},{2,18},{3,19},{4,20},{5,21},{6,22},{7,23},{8,24},{9,... | collective-permute-start | bytes 294920 | tf_op jit(solution)/shard_map/ppermute | solution.py:30
  14.3 12.5 %collective-permute-start.7 = (bf16[24,1,64,32]{3,0,2,1:T(8,128)(2,1)S(1)}, bf16[24,1,64,32]{3,0,2,1:T(8,128)(2,1)S(1)}, u32[]{:S(2)}, u32[]{:S(2)}) collective-permute-start(bf16[24,1,64,32]{3,0,2,1:T(8,128)(2,1)S(1)} %get-tuple-element.47), channel_id=1, source_target_pairs={{16,0},{17,1},{18,2},{19,3},{20,4},{21,5},{22,6},{23,7},{24,8},{25... | collective-permute-start | bytes 294920 | tf_op jit(solution)/shard_map/ppermute | solution.py:32
  15.6 85.7 %collective-permute-start = (bf16[4,64,320]{2,1,0:T(8,128)(2,1)S(1)}, bf16[4,64,320]{2,1,0:T(8,128)(2,1)}, u32[]{:S(2)}, u32[]{:S(2)}) collective-permute-start(bf16[4,64,320]{2,1,0:T(8,128)(2,1)S(1)} %copy-done.27), channel_id=1, source_target_pairs={{0,1},{1,2},{2,3},{3,4},{4,5},{5,6},{6,7},{7,8},{8,9},{9,10},{10,1... | collective-permute-start | bytes 491528 | tf_op jit(solution)/shard_map/ppermute | solution.py:19
  26.8 0.7 copy-start.23
  27.6 8.8 %collective-permute-start.8 = (bf16[24,6,1,32]{3,0,2,1:T(8,128)(2,1)S(1)}, bf16[24,6,1,32]{3,0,2,1:T(8,128)(2,1)S(1)}, u32[]{:S(2)}, u32[]{:S(2)}) collective-permute-start(bf16[24,6,1,32]{3,0,2,1:T(8,128)(2,1)S(1)} %get-tuple-element.20), channel_id=1, source_target_pairs={{0,1},{1,2},{2,3},{3,4},{4,5},{5,6},{6,7},{7,8},{8,9},{9,10},{10,1... | collective-permute-start | bytes 27656 | tf_op jit(solution)/shard_map/ppermute | solution.py:30
  28.9 7.6 %collective-permute-start.9 = (bf16[24,6,1,32]{3,0,2,1:T(8,128)(2,1)S(1)}, bf16[24,6,1,32]{3,0,2,1:T(8,128)(2,1)S(1)}, u32[]{:S(2)}, u32[]{:S(2)}) collective-permute-start(bf16[24,6,1,32]{3,0,2,1:T(8,128)(2,1)S(1)} %get-tuple-element.21), channel_id=1, source_target_pairs={{1,0},{2,1},{3,2},{4,3},{5,4},{6,5},{7,6},{8,7},{9,8},{10,9},{11,1... | collective-permute-start | bytes 27656 | tf_op jit(solution)/shard_map/ppermute | solution.py:32
  39.5 0.7 copy-start.29
  48.8 46.2 %copy-start.6 = (f32[4,64,320]{2,1,0:T(8,128)}, f32[4,64,320]{2,1,0:T(8,128)S(1)}, u32[]{:S(2)}) copy-start(f32[4,64,320]{2,1,0:T(8,128)S(1)} %fusion.112) | copy-start | bytes 983044
  49.2 45.8 %copy-start.8 = (f32[4,64,320]{2,1,0:T(8,128)}, f32[4,64,320]{2,1,0:T(8,128)S(1)}, u32[]{:S(2)}) copy-start(f32[4,64,320]{2,1,0:T(8,128)S(1)} %fusion.114) | copy-start | bytes 983044
  49.7 45.3 %copy-start.10 = (f32[4,64,320]{2,1,0:T(8,128)}, f32[4,64,320]{2,1,0:T(8,128)S(1)}, u32[]{:S(2)}) copy-start(f32[4,64,320]{2,1,0:T(8,128)S(1)} %fusion.116) | copy-start | bytes 983044
  101.1 7.5 %copy-start.5 = (f32[24,4,64,40]{2,3,1,0:T(8,128)S(1)}, f32[24,4,64,40]{2,3,1,0:T(8,128)}, u32[]{:S(2)}) copy-start(f32[24,4,64,40]{2,3,1,0:T(8,128)} %fusion.45) | copy-start | bytes 2949124
  101.4 6.2 %collective-permute-start.1 = (bf16[4,64,320]{2,1,0:T(8,128)(2,1)}, bf16[4,64,320]{2,1,0:T(8,128)(2,1)S(1)}, u32[]{:S(2)}, u32[]{:S(2)}) collective-permute-start(bf16[4,64,320]{2,1,0:T(8,128)(2,1)} %collective-permute-done), channel_id=1, source_target_pairs={{0,1},{1,2},{2,3},{3,4},{4,5},{5,6},{6,7},{7,8},{8,9},{9,10},{10,1... | collective-permute-start | bytes 491528 | tf_op jit(solution)/shard_map/ppermute | solution.py:19
  118.3 6.5 %copy-start.28 = (bf16[4,64,320]{2,1,0:T(8,128)(2,1)S(1)}, bf16[4,64,320]{2,1,0:T(8,128)(2,1)}, u32[]{:S(2)}) copy-start(bf16[4,64,320]{2,1,0:T(8,128)(2,1)} %param.5) | copy-start | bytes 491524
  118.8 6.0 %copy-start.26 = (f32[4,64,320]{2,1,0:T(8,128)S(1)}, f32[4,64,320]{2,1,0:T(8,128)}, u32[]{:S(2)}) copy-start(f32[4,64,320]{2,1,0:T(8,128)} %fusion.104) | copy-start | bytes 983044
  119.4 5.5 %copy-start.25 = (f32[4,64,320]{2,1,0:T(8,128)S(1)}, f32[4,64,320]{2,1,0:T(8,128)}, u32[]{:S(2)}) copy-start(f32[4,64,320]{2,1,0:T(8,128)} %fusion.102) | copy-start | bytes 983044
  119.9 5.0 %copy-start.22 = (f32[4,64,320]{2,1,0:T(8,128)S(1)}, f32[4,64,320]{2,1,0:T(8,128)}, u32[]{:S(2)}) copy-start(f32[4,64,320]{2,1,0:T(8,128)} %fusion.138) | copy-start | bytes 983044
  119.9 5.0 %copy-start.24 = (f32[4,64,320]{2,1,0:T(8,128)S(1)}, f32[4,64,320]{2,1,0:T(8,128)}, u32[]{:S(2)}) copy-start(f32[4,64,320]{2,1,0:T(8,128)} %fusion.100) | copy-start | bytes 983044
  120.4 4.5 %copy-start.21 = (f32[4,64,320]{2,1,0:T(8,128)S(1)}, f32[4,64,320]{2,1,0:T(8,128)}, u32[]{:S(2)}) copy-start(f32[4,64,320]{2,1,0:T(8,128)} %fusion.136) | copy-start | bytes 983044
  120.9 4.0 %copy-start.19 = (f32[4,64,320]{2,1,0:T(8,128)S(1)}, f32[4,64,320]{2,1,0:T(8,128)}, u32[]{:S(2)}) copy-start(f32[4,64,320]{2,1,0:T(8,128)} %fusion.132) | copy-start | bytes 983044
  121.0 4.0 %copy-start.20 = (f32[4,64,320]{2,1,0:T(8,128)S(1)}, f32[4,64,320]{2,1,0:T(8,128)}, u32[]{:S(2)}) copy-start(f32[4,64,320]{2,1,0:T(8,128)} %fusion.134) | copy-start | bytes 983044
  121.5 3.5 copy-start.7
  121.5 3.5 copy-start.9
  121.5 3.5 copy-start.11
  121.5 3.5 copy-start.12
  121.5 3.5 copy-start.13
  121.5 3.5 copy-start.14
  121.5 3.5 copy-start.15
  121.6 3.5 copy-start.16
  121.6 3.5 copy-start.17
  121.6 3.5 copy-start.18
  121.8 7.7 %collective-permute-start.2 = (bf16[24,1,64,40]{2,3,1,0:T(8,128)(2,1)S(1)}, bf16[24,1,64,40]{2,3,1,0:T(8,128)(2,1)S(1)}, u32[]{:S(2)}, u32[]{:S(2)}) collective-permute-start(bf16[24,1,64,40]{2,3,1,0:T(8,128)(2,1)S(1)} %get-tuple-element.50), channel_id=1, source_target_pairs={{0,16},{1,17},{2,18},{3,19},{4,20},{5,21},{6,22},{7,23},{8,24},{9,... | collective-permute-start | bytes 368648 | tf_op jit(solution)/shard_map/ppermute | solution.py:30
  123.6 8.4 %collective-permute-start.3 = (bf16[24,1,64,40]{2,3,1,0:T(8,128)(2,1)S(1)}, bf16[24,1,64,40]{2,3,1,0:T(8,128)(2,1)S(1)}, u32[]{:S(2)}, u32[]{:S(2)}) collective-permute-start(bf16[24,1,64,40]{2,3,1,0:T(8,128)(2,1)S(1)} %get-tuple-element.51), channel_id=1, source_target_pairs={{16,0},{17,1},{18,2},{19,3},{20,4},{21,5},{22,6},{23,7},{24,8},{25... | collective-permute-start | bytes 368648 | tf_op jit(solution)/shard_map/ppermute | solution.py:32
  136.4 12.9 %collective-permute-start.4 = (bf16[24,6,1,40]{3,0,2,1:T(8,128)(2,1)S(1)}, bf16[24,6,1,40]{3,0,2,1:T(8,128)(2,1)S(1)}, u32[]{:S(2)}, u32[]{:S(2)}) collective-permute-start(bf16[24,6,1,40]{3,0,2,1:T(8,128)(2,1)S(1)} %copy.202), channel_id=1, source_target_pairs={{0,1},{1,2},{2,3},{3,4},{4,5},{5,6},{6,7},{7,8},{8,9},{9,10},{10,1... | collective-permute-start | bytes 34568 | tf_op jit(solution)/shard_map/ppermute | solution.py:30
  141.6 8.7 %collective-permute-start.5 = (bf16[24,6,1,40]{3,0,2,1:T(8,128)(2,1)S(1)}, bf16[24,6,1,40]{3,0,2,1:T(8,128)(2,1)S(1)}, u32[]{:S(2)}, u32[]{:S(2)}) collective-permute-start(bf16[24,6,1,40]{3,0,2,1:T(8,128)(2,1)S(1)} %copy.203), channel_id=1, source_target_pairs={{1,0},{2,1},{3,2},{4,3},{5,4},{6,5},{7,6},{8,7},{9,8},{10,9},{11,1... | collective-permute-start | bytes 34568 | tf_op jit(solution)/shard_map/ppermute | solution.py:32
  147.2 2.1 copy-start.2
  148.0 78.6 %collective-permute-start.10 = (f32[4,64,320]{2,1,0:T(8,128)}, f32[4,64,320]{2,1,0:T(8,128)}, u32[]{:S(2)}, u32[]{:S(2)}) collective-permute-start(f32[4,64,320]{2,1,0:T(8,128)} %slice.426), channel_id=1, source_target_pairs={{1,0},{2,1},{3,2},{4,3},{5,4},{6,5},{7,6},{8,7},{9,8},{10,9},{11,1... | collective-permute-start | bytes 983048 | tf_op jit(solution)/shard_map/ppermute | solution.py:19
  225.9 1.3 copy-start.3
  229.0 117.5 %collective-permute-start.11 = (f32[4,64,320]{2,1,0:T(8,128)}, f32[4,64,320]{2,1,0:T(8,128)}, u32[]{:S(2)}, u32[]{:S(2)}) collective-permute-start(f32[4,64,320]{2,1,0:T(8,128)} %slice_add_fusion.1), channel_id=1, source_target_pairs={{1,0},{2,1},{3,2},{4,3},{5,4},{6,5},{7,6},{8,7},{9,8},{10,9},{11,1... | collective-permute-start | bytes 983048 | tf_op jit(solution)/shard_map/ppermute | solution.py:19
Sparse Core Ops, SparseCore 0:
  211.9 132.7 all-reduce.26
where the time goes:
time: 361 us; the launch traced here: 355 us
  waiting for transfers between devices  124 us (34%)
  matrix products  93 us (26%)
  local copies, waits for them, and re-layouts  74 us (20%)
  starting transfers between devices  27.5 us (8%)
  other arithmetic  20.8 us (6%)
  between operations  15.6 us (4%)
    psum x1, waiting for transfers between devices, on_device(): weight_grad = lax.psum(local_grad, ('row', 'col')) / math.sqrt(total_cells)  112 us
    transpose x1, matrix products, on_device(): local_grad = jnp.transpose(kernel_raw, (1, 2, 3, 0, 4))  42.7 us
    dot_general x24, matrix products, on_device(): jnp.einsum('hwg,cg->hwc', grad_volume[disp_index].astype(jnp.float32), gr...  25.2 us
    convert_element_type x50, local copies, waits for them, and re-layouts, on_device(): grad_volume = conv_valid(padded_cotangent, flipped).astype(jnp.bfloat16)  21.1 us
    unnamed x88, local copies, waits for them, and re-layouts  20.9 us
    broadcast_in_dim x2, local copies, waits for them, and re-layouts, on_device(): full_pad[None]  13.9 us
    dot_general x24, matrix products, on_device(): jnp.einsum('hwc,cg->hwg', left_float * shifted, group_table, precision=la...  13.7 us
    ppermute x4, starting transfers between devices, with_halo(): lax.ppermute(tail, axis, [(i, (i + 1) % count) for i in range(ends)])  12.3 us
  transfers between devices with their start and end apart: 13, of which 5 were waited for; matrix products, arithmetic and copies ran while one was open for 46% of the time, Pallas kernels for 0%

commit v1 on v0

v1 whole, which is shorter than its diff:
```python
import functools
import math

import jax
import jax.numpy as jnp
from jax import lax
from jax.experimental import pallas as pl
from jax.experimental.pallas import tpu as pltpu
from jax.sharding import PartitionSpec as P

DISP = 24
STEP = 4
SLOT = 64
PAD = 8
F32 = jnp.float32
BF16 = jnp.bfloat16
VMEM = pl.BlockSpec(memory_space=pltpu.VMEM)
LIMIT = 40 * 1024 * 1024


def params():
    return pltpu.CompilerParams(vmem_limit_bytes=LIMIT)


def lanes(shape):
    return lax.broadcasted_iota(jnp.int32, shape, len(shape) - 1)


def channel_table(channels, group_size, flip):
    shape = (group_size * SLOT, channels) if flip else (channels, group_size * SLOT)
    c = lax.broadcasted_iota(jnp.int32, shape, 1 if flip else 0)
    j = lax.broadcasted_iota(jnp.int32, shape, 0 if flip else 1)
    hit = (lax.rem(c, group_size) == lax.div(j, SLOT)) & (lax.div(c, group_size) == lax.rem(j, SLOT))
    return jnp.where(hit, 1.0, 0.0).astype(BF16)


def dot(a, b):
    return jnp.dot(a, b, preferred_element_type=F32)


def pack_kernel(ends, left, right, ct, r1, r2, c1, ctl, *rest):
    n = len(ends)
    row_refs, lo_refs, hi_refs = rest[:n], rest[n : 2 * n], rest[2 * n : 3 * n]
    ctf, rowf = rest[3 * n :]
    disp, rows, cols, feat = ct.shape
    for h in range(rows):
        r1[h * cols : (h + 1) * cols] = right[h]
        r2[h * (cols // 2) : (h + 1) * (cols // 2)] = right[h, cols // 2 :]
    for d in range(disp):
        block = jnp.concatenate([ct[d, h].astype(F32) for h in range(rows)], axis=1)
        ctf[d * cols : (d + 1) * cols] = block
        ctl[d] = block.astype(BF16)
    width = rows * feat
    for ref, base, col in ((r1, rows * cols, cols - 1), (c1, 0, 0)):
        ref[base : base + 32] = jnp.zeros((32, ref.shape[1]), BF16)
        ref[base : base + disp, 0:width] = ctf[pl.ds(col, disp, stride=cols), :].astype(BF16)
        edge = [left[h, col : col + 1].astype(F32) for h in range(rows)]
        edge += [right[h, col : col + 1].astype(F32) for h in range(rows)]
        ref[base + disp : base + 32] = jnp.concatenate(edge, axis=0).astype(BF16)
    per = 128 // feat
    for end, row_ref, lo_ref, hi_ref in zip(ends, row_refs, lo_refs, hi_refs):
        h = end()
        for q in range(disp // per):
            rowf[q * cols : (q + 1) * cols] = jnp.concatenate(
                [ct[q * per + i, h].astype(F32) for i in range(per)], axis=1
            )
        row_ref[...] = rowf[...].astype(BF16)
        for ref, col in ((lo_ref, 0), (hi_ref, cols - 1)):
            ref[...] = jnp.zeros(ref.shape, BF16)
            ref[0 : disp // per] = rowf[pl.ds(col, disp // per, stride=cols), :].astype(BF16)


def volume_kernel(ends, group_size, left, right, r1, r2, c1, vsh, fl, fr, fr4, *rest):
    pays, vbuf = rest[: len(ends)], rest[len(ends)]
    rows, cols, channels = left.shape
    disp = vsh.shape[0] - 2
    reach = fr.shape[1] - cols - PAD
    table = channel_table(channels, group_size, False)
    wide = group_size * SLOT

    def spread(x):
        return dot(x, table)

    base = rows * cols
    edge_l = spread(r1[base : base + 32])
    edge_r = spread(c1[...])
    far = spread(r2[...])
    near = spread(r1[0:base])
    own = spread(right[...].reshape(base, channels))
    own_l = spread(left[...].reshape(base, channels))
    half = cols // 2
    for h in range(rows):
        fl[h, 0:PAD] = jnp.zeros((PAD, wide), F32)
        fl[h, PAD + cols :] = jnp.zeros((PAD, wide), F32)
        fl[h, PAD - 1 : PAD] = edge_l[disp + h : disp + h + 1]
        fl[h, PAD : PAD + cols] = own_l[h * cols : (h + 1) * cols]
        fl[h, PAD + cols : PAD + cols + 1] = edge_r[disp + h : disp + h + 1]
        for ref, off in ((fr, 0), (fr4, STEP)):
            start = reach - cols - half + off
            ref[h, 0:start] = jnp.zeros((start, wide), F32)
            ref[h, start : start + half] = far[h * half : (h + 1) * half]
            ref[h, start + half : start + half + cols] = near[h * cols : (h + 1) * cols]
            ref[h, start + half + cols : start + half + 2 * cols] = own[h * cols : (h + 1) * cols]
            tail = ref.shape[1] - (start + half + 2 * cols)
            ref[h, start + half + 2 * cols :] = jnp.zeros((tail, wide), F32)
            ref[h, start + half + 2 * cols : start + half + 2 * cols + 1] = edge_r[
                disp + rows + h : disp + rows + h + 1
            ]
    vsh[0] = jnp.zeros(vsh.shape[1:], BF16)
    vsh[disp + 1] = jnp.zeros(vsh.shape[1:], BF16)
    total = cols + 2 * PAD
    block = 16
    low = lanes((block, 128)) < SLOT
    scale = 1.0 / group_size

    def pair(dd, _):
        for odd in range(2):
            band = fr4 if odd else fr
            for b in range(total // block):
                at = pl.multiple_of(reach - PAD + b * block - 2 * STEP * dd, 8)
                sums = []
                for h in range(rows):
                    prod = fl[h, b * block : (b + 1) * block] * band[h, pl.ds(at, block)]
                    acc = prod[:, 0:128]
                    for j in range(1, wide // 128):
                        acc = acc + prod[:, 128 * j : 128 * (j + 1)]
                    sums.append((acc + pltpu.roll(acc, SLOT, 1)) * scale)
                for p in range(rows // 2):
                    vbuf[odd, b * block : (b + 1) * block, 128 * p : 128 * (p + 1)] = jnp.where(
                        low, sums[2 * p], sums[2 * p + 1]
                    )
            for e in range(3):
                vsh[2 * dd + odd + 1, :, 256 * e : 256 * (e + 1)] = vbuf[
                    odd, PAD - 1 + e : PAD - 1 + e + cols
                ].astype(BF16)
        big = lanes((total, 128)) < SLOT
        for end, pay in zip(ends, pays):
            h = end()
            if isinstance(h, int):
                lane = 128 * (h // 2)
                halves = [vbuf[o, :, lane : lane + 128] for o in range(2)]
                if h % 2 == 0:
                    halves[1] = pltpu.roll(halves[1], SLOT, 1)
                else:
                    halves[0] = pltpu.roll(halves[0], SLOT, 1)
                out = jnp.where(big, halves[0], halves[1])
            else:
                first = jnp.where(big, vbuf[0, :, 0:128], pltpu.roll(vbuf[1, :, 0:128], SLOT, 1))
                last = jnp.where(
                    big, pltpu.roll(vbuf[0, :, 128:256], SLOT, 1), vbuf[1, :, 128:256]
                )
                out = jnp.where(h == 0, first, last)
            pay[dd] = out.astype(BF16)
        return 0

    lax.fori_loop(0, disp // 2, pair, 0)


def weight_kernel(
    masks, groups, vsh, ctl, r1, c1, top, bot, tl, bl, tr, br, pay, ctsh, vt, buf, edges
):
    disp, cols, width = ctl.shape
    rows, feat = vsh.shape[2] // 3 // SLOT, 32
    per = 128 // feat
    mtop, mbot = masks()
    first = lanes((8, 128))
    base = r1.shape[0] - 32
    for side, (main, at, t, b) in enumerate(((r1, base, tl, bl), (c1, 0, tr, br))):
        edges[2 * side] = main[at : at + disp, 0:128].astype(F32)
        tv = t[0:8].astype(F32) * mtop
        bv = b[0:8].astype(F32) * mbot
        for i in range(per):
            a = tv if i == 0 else pltpu.roll(tv, 128 - feat * i, 1)
            z = pltpu.roll(bv, (128 + feat - feat * i) % 128, 1) if i != 1 else bv
            val = jnp.where(first < feat, a, jnp.where(first < 2 * feat, z, 0.0))
            edges[2 * side + 1, pl.ds(i, disp // per, stride=per)] = val[0 : disp // per]
    ctsh[0] = jnp.zeros(ctsh.shape[1:], BF16)
    ctsh[disp + 1] = jnp.zeros(ctsh.shape[1:], BF16)
    lane = lanes((cols, 128))

    def fill(q, _):
        t = top[pl.ds(pl.multiple_of(q * cols, cols), cols)].astype(F32) * mtop
        z = bot[pl.ds(pl.multiple_of(q * cols, cols), cols)].astype(F32) * mbot
        for i in range(per):
            d = q * per + i
            a = t if i == 0 else pltpu.roll(t, 128 - feat * i, 1)
            y = z if i == 1 else pltpu.roll(z, (128 + feat - feat * i) % 128, 1)
            buf[i, PAD : PAD + cols, 0:128] = ctl[d].astype(F32)
            buf[i, PAD : PAD + cols, 128:256] = jnp.where(
                lane < feat, a, jnp.where(lane < 2 * feat, y, 0.0)
            )
            for part in range(2):
                at = slice(128 * part, 128 * (part + 1))
                buf[i, PAD - 1 : PAD, at] = edges[part, pl.ds(d, 1)]
                buf[i, PAD + cols : PAD + cols + 1, at] = edges[2 + part, pl.ds(d, 1)]
            for e in range(3):
                ctsh[d + 1, :, 256 * e : 256 * (e + 1)] = buf[
                    i, PAD - 1 + e : PAD - 1 + e + cols
                ].astype(BF16)
        return 0

    lax.fori_loop(0, disp // per, fill, 0)
    step = 256 // cols
    for q in range(disp // step):
        v = vsh[1 + q * step : 1 + (q + 1) * step, :, 256:512].reshape(256, 256)
        vt[:, 256 * q : 256 * (q + 1)] = v.T
    keep = lanes((groups, 128))

    def taps(a, _):
        for e in range(3):
            ct_block = ctsh[pl.ds(a, disp), :, 256 * e : 256 * (e + 1)].reshape(disp * cols, 256)
            full = dot(vt[...], ct_block)
            out = None
            for h in range(rows):
                x = full[SLOT * h : SLOT * h + groups, 0:128]
                y = full[SLOT * h : SLOT * h + groups, 128:256]
                if h == 0:
                    term = jnp.where(keep < feat, y, pltpu.roll(x, feat, 1))
                else:
                    term = x if h == 1 else pltpu.roll(x, 128 - feat * (h - 1), 1)
                    if h == rows - 1:
                        term = jnp.where(keep < 2 * feat, term, pltpu.roll(y, feat, 1))
                out = term if out is None else out + term
            pay[a, groups * e : groups * (e + 1)] = jnp.where(keep < 3 * feat, out, 0.0).astype(BF16)
        return 0

    lax.fori_loop(0, 3, taps, 0)


def feature_kernel(group_size, ctsh, w2, fl, fr, fr4, lg, rg0, rg1, rg2, gv, accl, accr):
    disp = ctsh.shape[0] - 2
    rows, cols, channels = lg.shape
    reach = fr.shape[1] - cols - PAD
    wide = group_size * SLOT
    step = 256 // cols
    low = lanes((256, 128)) < SLOT
    scale = 1.0 / group_size
    for h in range(rows):
        gv[h, :, 0:PAD] = jnp.zeros((disp, PAD, 128), F32)
        gv[h, :, PAD + cols :] = jnp.zeros((disp, PAD, 128), F32)

    def conv(q, _):
        acc = None
        for a in range(3):
            block = ctsh[pl.ds(q * step + a, step)].reshape(256, ctsh.shape[2])
            part = dot(block, w2[a])
            acc = part if acc is None else acc + part
        g = acc.astype(BF16).astype(F32) * scale
        for p in range(rows // 2):
            x = g[:, 128 * p : 128 * (p + 1)]
            r = pltpu.roll(x, SLOT, 1)
            for o in range(2):
                y = jnp.where(low, r, x) if o else jnp.where(low, x, r)
                gv[2 * p + o, pl.ds(q * step, step), PAD : PAD + cols] = y.reshape(step, cols, 128)
        return 0

    lax.fori_loop(0, disp // step, conv, 0)

    def left_block(i, _):
        h = lax.div(i, cols // 8)
        w = pl.multiple_of(lax.rem(i, cols // 8) * 8, 8)
        accs = [jnp.zeros((8, 128), F32) for _ in range(wide // 128)]
        for d in range(disp):
            band = fr4 if d % 2 else fr
            at = pl.multiple_of(w + reach - 2 * STEP * (d // 2), 8)
            g = gv[h, d, pl.ds(w + PAD, 8)]
            for j in range(wide // 128):
                accs[j] = accs[j] + g * band[h, pl.ds(at, 8), 128 * j : 128 * (j + 1)]
        for j in range(wide // 128):
            accl[h, pl.ds(w, 8), 128 * j : 128 * (j + 1)] = accs[j]
        return 0

    lax.fori_loop(0, rows * (cols // 8), left_block, 0)
    back = accr.shape[1] - cols

    def right_row(h, _):
        for u in range(-back, cols, 8):
            accs = [jnp.zeros((8, 128), F32) for _ in range(wide // 128)]
            for d in range(disp):
                w = u + STEP * d
                if w <= -8 or w >= cols:
                    continue
                g = gv[h, d, w + PAD : w + PAD + 8]
                for j in range(wide // 128):
                    accs[j] = accs[j] + g * fl[h, w + PAD : w + PAD + 8, 128 * j : 128 * (j + 1)]
            for j in range(wide // 128):
                accr[h, u + back : u + back + 8, 128 * j : 128 * (j + 1)] = accs[j]
        return 0

    lax.fori_loop(0, rows, right_row, 0)
    table = channel_table(channels, group_size, True)
    half = cols // 2
    for h in range(rows):
        lg[h] = dot(accl[h].astype(BF16), table).astype(BF16)
        whole = dot(accr[h].astype(BF16), table).astype(BF16)
        rg2[h] = whole[back - cols - half : back - cols]
        rg1[h] = whole[back - cols : back]
        rg0[h] = whole[back:]


def conv_kernel(masks, vsh, top, bot, wc, wh, out, halo, buf):
    disp, rows, cols, feat = out.shape
    mtop, mbot = masks()
    total = top.shape[1]
    low = lanes((total, 128)) < SLOT
    halo[0] = jnp.zeros(halo.shape[1:], BF16)
    halo[disp + 1] = jnp.zeros(halo.shape[1:], BF16)

    def fill(dd, _):
        t = top[dd].astype(F32) * mtop
        b = bot[dd].astype(F32) * mbot
        buf[0] = jnp.where(low, t, pltpu.roll(b, SLOT, 1))
        buf[1] = jnp.where(low, pltpu.roll(t, SLOT, 1), b)
        for o in range(2):
            for e in range(3):
                halo[2 * dd + o + 1, :, 128 * e : 128 * (e + 1)] = buf[
                    o, PAD - 1 + e : PAD - 1 + e + cols
                ].astype(BF16)
        return 0

    lax.fori_loop(0, disp // 2, fill, 0)
    step = 256 // cols

    def conv(q, _):
        acc = None
        for a in range(3):
            main = vsh[pl.ds(q * step + a, step)].reshape(256, vsh.shape[2])
            side = halo[pl.ds(q * step + a, step)].reshape(256, halo.shape[2])
            part = dot(main, wc[a]) + dot(side, wh[a])
            acc = part if acc is None else acc + part
        for i in range(step):
            for h in range(rows):
                out[q * step + i, h] = acc[
                    i * cols : (i + 1) * cols, feat * h : feat * (h + 1)
                ].astype(BF16)
        return 0

    lax.fori_loop(0, disp // step, conv, 0)


def finish_weight_kernel(scale, one, two, out):
    _, _, _, groups, feat = out.shape
    for a in range(3):
        for e in range(3):
            at = groups * e
            x = (one[a, at : at + groups].astype(F32) + two[a, at : at + groups].astype(F32)) * scale
            for b in range(3):
                out[2 - a, 2 - b, 2 - e] = x[:, feat * b : feat * (b + 1)]


def finish_right_kernel(own, near, far, out):
    rows, cols, channels = out.shape
    half = cols // 2
    for h in range(rows):
        total = own[h].astype(F32) + near[h].astype(F32)
        out[h, 0:half] = total[0:half].astype(BF16)
        out[h, half:] = (total[half:] + far[h].astype(F32)).astype(BF16)


def call(kernel, outs, scratch, *args):
    return pl.pallas_call(
        kernel,
        out_shape=[jax.ShapeDtypeStruct(s, t) for s, t in outs],
        in_specs=[VMEM] * len(args),
        out_specs=[VMEM] * len(outs),
        scratch_shapes=scratch,
        compiler_params=params(),
    )(*args)


def col_shift(block, distance):
    n = lax.axis_size("col")
    route = [(i - distance, i) for i in range(n) if 0 <= i - distance < n]
    return lax.ppermute(block, "col", route)


def grid_shift(block, down, distance):
    rows, n = lax.axis_size("row"), lax.axis_size("col")
    route = []
    for r in range(rows):
        for c in range(n):
            if 0 <= r - down < rows and 0 <= c - distance < n:
                route.append(((r - down) * n + c - distance, r * n + c))
    return lax.ppermute(block, ("row", "col"), route)


def grid_swap(block, distance):
    n = lax.axis_size("col")
    route = [
        ((1 - r) * n + c - distance, r * n + c)
        for r in range(2)
        for c in range(n)
        if 0 <= c - distance < n
    ]
    return lax.ppermute(block, ("row", "col"), route)


def halos(pays, distance):
    if lax.axis_size("row") == 2:
        got = grid_swap(pays[0], distance)
        return got, got
    return grid_shift(pays[0], 1, distance), grid_shift(pays[1], -1, distance)


def banded(conv_weight, rows):
    _, _, _, groups, _ = conv_weight.shape
    padded = jnp.pad(conv_weight, ((0, 0), (rows - 1, rows - 1), (0, 0), (0, SLOT - groups), (0, 0)))
    stack = [padded[:, rows - 1 - h : 2 * rows + 1 - h] for h in range(rows)]
    return jnp.stack(stack, axis=4).transpose(0, 2, 1, 3, 4, 5)


def on_device(left_features, right_features, conv_weight, cotangent):
    rows, cols, channels = left_features.shape
    disp, feat = cotangent.shape[0], cotangent.shape[3]
    groups = conv_weight.shape[3]
    group_size = channels // groups
    wide = group_size * SLOT
    n_row, n_col = lax.axis_size("row"), lax.axis_size("col")
    per = 128 // feat

    if n_row == 2:
        ends = [lambda: (rows - 1) * (1 - lax.axis_index("row"))]
    else:
        ends = [lambda: rows - 1, lambda: 0]
    n = len(ends)

    def masks():
        at = lax.axis_index("row")
        return (
            jnp.where(at > 0, 1.0, 0.0).astype(F32),
            jnp.where(at < n_row - 1, 1.0, 0.0).astype(F32),
        )

    packed = call(
        functools.partial(pack_kernel, ends),
        [
            ((rows * cols + 32, channels), BF16),
            ((rows * cols // 2, channels), BF16),
            ((32, channels), BF16),
            ((disp, cols, rows * feat), BF16),
        ]
        + [((disp // per * cols, 128), BF16)] * n
        + [((16, 128), BF16)] * (2 * n),
        [pltpu.VMEM((disp * cols, rows * feat), F32), pltpu.VMEM((disp // per * cols, 128), F32)],
        left_features,
        right_features,
        cotangent,
    )
    r1, r2, c1, ctl = packed[:4]
    row_pay, lo_pay, hi_pay = packed[4 : 4 + n], packed[4 + n : 4 + 2 * n], packed[4 + 2 * n :]
    r1 = col_shift(r1, 1)
    top, bot = halos(row_pay, 0)
    r2 = col_shift(r2, 2)
    c1 = col_shift(c1, -1)
    tl, bl = halos(hi_pay, 1)
    tr, br = halos(lo_pay, -1)

    six = banded(conv_weight, rows)
    wc = six[:, :, 1 : rows + 1].reshape(3, 3 * rows * SLOT, rows * feat)
    wh = jnp.concatenate([six[:, :, :1], six[:, :, rows + 1 :]], axis=2)
    wh = wh.reshape(3, 3 * 2 * SLOT, rows * feat)
    back = banded(conv_weight[::-1, ::-1, ::-1], rows)
    back = jnp.concatenate([back[:, :, 1 : rows + 1], back[:, :, :1], back[:, :, rows + 1 :]], axis=2)
    back = back.transpose(0, 1, 2, 5, 4, 3).reshape(3, 3, (rows + 2) * feat, rows * SLOT)
    w2 = jnp.pad(back, ((0, 0), (0, 0), (0, 256 - (rows + 2) * feat), (0, 0)))
    w2 = w2.reshape(3, 3 * 256, rows * SLOT)

    band = 104 + cols + PAD
    volume = call(
        functools.partial(volume_kernel, ends, group_size),
        [
            ((disp + 2, cols, 3 * rows * SLOT), BF16),
            ((rows, cols + 2 * PAD, wide), F32),
            ((rows, band, wide), F32),
            ((rows, band, wide), F32),
        ]
        + [((disp // 2, cols + 2 * PAD, 128), BF16)] * n,
        [pltpu.VMEM((2, cols + 2 * PAD, rows * SLOT), F32)],
        left_features,
        right_features,
        r1,
        r2,
        c1,
    )
    vsh, fl, fr, fr4 = volume[:4]
    vtop, vbot = halos(volume[4:], 0)

    part, ctsh = call(
        functools.partial(weight_kernel, masks, groups),
        [((3, 3 * groups, 128), BF16), ((disp + 2, cols, 3 * 256), BF16)],
        [
            pltpu.VMEM((rows * SLOT, disp * cols), BF16),
            pltpu.VMEM((per, cols + 2 * PAD, 256), F32),
            pltpu.VMEM((4, disp, 128), F32),
        ],
        vsh, ctl, r1, c1, top, bot, tl, bl, tr, br,
    )

    hops = []
    for axis, size in (("col", n_col), ("row", n_row)):
        bit = 1
        while bit < size:
            hops.append((axis, [(i, i ^ bit) for i in range(size)]))
            bit *= 2
    for step, (axis, route) in enumerate(hops):
        other = lax.ppermute(part, axis, route)
        if step < len(hops) - 1:
            part = (part.astype(F32) + other.astype(F32)).astype(BF16)
    cells = disp * rows * n_row * cols * n_col

    lg, rg0, rg1, rg2 = call(
        functools.partial(feature_kernel, group_size),
        [
            ((rows, cols, channels), BF16),
            ((rows, cols, channels), BF16),
            ((rows, cols, channels), BF16),
            ((rows, cols // 2, channels), BF16),
        ],
        [
            pltpu.VMEM((rows, disp, cols + 2 * PAD, 128), F32),
            pltpu.VMEM((rows, cols, wide), F32),
            pltpu.VMEM((rows, cols + cols + cols // 2, wide), F32),
        ],
        ctsh, w2, fl, fr, fr4,
    )
    rg1 = col_shift(rg1, -1)
    rg2 = col_shift(rg2, -2)

    (output,) = call(
        functools.partial(conv_kernel, masks),
        [((disp, rows, cols, feat), BF16)],
        [
            pltpu.VMEM((disp + 2, cols, 3 * 2 * SLOT), BF16),
            pltpu.VMEM((2, cols + 2 * PAD, 128), F32),
        ],
        vsh, vtop, vbot, wc, wh,
    )
    (right_grad,) = call(
        finish_right_kernel, [((rows, cols, channels), BF16)], [], rg0, rg1, rg2
    )
    (weight_grad,) = call(
        functools.partial(finish_weight_kernel, 1.0 / math.sqrt(cells)),
        [(conv_weight.shape, F32)],
        [],
        part,
        other,
    )
    return (output, weight_grad, lg, right_grad)


def solution(mesh):
    in_specs = (P("row", "col", None), P("row", "col", None), P(), P(None, "row", "col", None))
    out_specs = (P(None, "row", "col", None), P(), P("row", "col", None), P("row", "col", None))
    return jax.shard_map(
        on_device, mesh=mesh, in_specs=in_specs, out_specs=out_specs, check_vma=False
    )
```

time: 361 us -> 108 us (0.30); the launches traced: 355 us -> 106 us
  waiting for transfers between devices: 124 us -> 3.17 us
  matrix products: 93 us -> 0 us
  local copies, waits for them, and re-layouts: 74 us -> 40.6 us
  Pallas kernels: 0 us -> 25.6 us
  other arithmetic: 20.8 us -> 4.74 us
  between operations: 15.6 us -> 0.98 us
  starting transfers between devices: 27.5 us -> 31.4 us
    psum x1 -> x0, waiting for transfers between devices: 112 us -> none  [on_device(): weight_grad = lax.psum(local_grad, ('row', 'col')) / math.sqrt(total_cells)]
    transpose x1 -> x0, matrix products: 42.7 us -> none  [on_device(): local_grad = jnp.transpose(kernel_raw, (1, 2, 3, 0, 4))]
    dot_general x48 -> x0, matrix products: 38.9 us -> none  [the longest x24 25.2 us: on_device(): jnp.einsum('hwg,cg->hwc', grad_volume[disp_index].astype(jnp.float32), gr...]
    pallas_call x0 -> x7, Pallas kernels: none -> 25.6 us  [call(): pl.pallas_call(kernel, out_shape=[jax.ShapeDtypeStruct(s, t) for s, t in...]
    convert_element_type x52 -> x0, local copies, waits for them, and re-layouts: 22.1 us -> none  [the longest x50 21.1 us: on_device(): grad_volume = conv_valid(padded_cotangent, flipped).astype(jnp.bfloat16)]
    broadcast_in_dim x5 -> x0, local copies, waits for them, and re-layouts: 20 us -> none  [the longest x2 13.9 us: on_device(): full_pad[None]]
    reshape x0 -> x5, local copies, waits for them, and re-layouts: none -> 11.6 us  [the longest x2 4.29 us: on_device(): wc = six[:, :, 1:rows + 1].reshape(3, 3 * rows * SLOT, rows * feat)]
    conv_general_dilated x2 -> x0, matrix products: 11.3 us -> none  [conv_valid(): lax.conv_general_dilated(padded_input[None], kernel, (1, 1, 1), ((1, 1),...]
  transfers between devices with their start and end apart: 13 -> 14, of which waited for: 5 -> 2; matrix products, arithmetic and copies ran while one was open for 46% -> 28% of each run, Pallas kernels for 0% -> 19%
where the time goes in v1:
time: 108 us; the launch traced here: 106 us
  local copies, waits for them, and re-layouts  40.6 us (38%)
  starting transfers between devices  31.4 us (29%)
  Pallas kernels  25.6 us (24%)
  other arithmetic  4.74 us (4%)
  waiting for transfers between devices  3.17 us (3%)
    pallas_call x7, Pallas kernels, call(): pl.pallas_call(kernel, out_shape=[jax.ShapeDtypeStruct(s, t) for s, t in...  25.6 us
    unnamed x45, local copies, waits for them, and re-layouts  16.3 us
    ppermute x5, starting transfers between devices, on_device(): other = lax.ppermute(part, axis, route)  13.4 us
    ppermute x5, starting transfers between devices, col_shift(): return lax.ppermute(block, 'col', route)  10.8 us
    ppermute x4, starting transfers between devices, grid_swap(): return lax.ppermute(block, ('row', 'col'), route)  7.17 us
    reshape x2, local copies, waits for them, and re-layouts, on_device(): wc = six[:, :, 1:rows + 1].reshape(3, 3 * rows * SLOT, rows * feat)  4.29 us
    reshape x1, local copies, waits for them, and re-layouts, on_device(): back.transpose(0, 1, 2, 5, 4, 3)  3.88 us
    reshape x2, local copies, waits for them, and re-layouts, on_device(): wh = wh.reshape(3, 3 * 2 * SLOT, rows * feat)  3.39 us
  transfers between devices with their start and end apart: 14, of which 2 were waited for; matrix products, arithmetic and copies ran while one was open for 28% of the time, Pallas kernels for 19%

profile of v1, /device:TPU:0, one launch (start us, length us, event | category | flops | bytes accessed | tf_op | source)
XLA Modules:
  0.0 106.4 jit_solution(11821214895734976010)
XLA Ops:
  0.7 0.0 copy-start.18
  0.7 1.8 %copy.13.ct = bf16[24,4,64,32]{3,2,1,0:T(8,128)(2,1)S(1)} copy(bf16[24,4,64,32]{2,3,1,0:T(8,128)(2,1)} %param.7) | data formatting | bytes 786432 | tf_op args[3]
  2.5 0.5 shard_map.75
  3.0 0.0 copy-start.11
  3.1 2.4 %collective-permute-start = (bf16[288,320]{1,0:T(8,128)(2,1)S(1)}, bf16[288,320]{1,0:T(8,128)(2,1)S(1)}, u32[]{:S(2)}, u32[]{:S(2)}) collective-permute-start(bf16[288,320]{1,0:T(8,128)(2,1)S(1)} %get-tuple-element.22), channel_id=1, source_target_pairs={{0,1},{1,2},{2,3},{3,4},{4,5},{5,6},{6,7},{7,8},{8,9},{9,10},{10,1... | collective-permute-start | bytes 552968 | tf_op jit(solution)/shard_map/ppermute | solution.py:374
  5.4 4.4 %collective-permute-start.1 = (bf16[128,320]{1,0:T(8,128)(2,1)S(1)}, bf16[128,320]{1,0:T(8,128)(2,1)S(1)}, u32[]{:S(2)}, u32[]{:S(2)}) collective-permute-start(bf16[128,320]{1,0:T(8,128)(2,1)S(1)} %get-tuple-element.23), channel_id=1, source_target_pairs={{0,2},{1,3},{2,4},{3,5},{4,6},{5,7},{6,8},{7,9},{8,10},{9,11},{10,... | collective-permute-start | bytes 245768 | tf_op jit(solution)/shard_map/ppermute | solution.py:374
  9.9 1.3 %collective-permute-start.2 = (bf16[32,320]{1,0:T(8,128)(2,1)S(1)}, bf16[32,320]{1,0:T(8,128)(2,1)S(1)}, u32[]{:S(2)}, u32[]{:S(2)}) collective-permute-start(bf16[32,320]{1,0:T(8,128)(2,1)S(1)} %get-tuple-element.24), channel_id=1, source_target_pairs={{1,0},{2,1},{3,2},{4,3},{5,4},{6,5},{7,6},{8,7},{9,8},{10,9},{11,1... | collective-permute-start | bytes 61448 | tf_op jit(solution)/shard_map/ppermute | solution.py:374
  11.2 1.6 %collective-permute-start.4 = (bf16[384,128]{1,0:T(8,128)(2,1)S(1)}, bf16[384,128]{1,0:T(8,128)(2,1)S(1)}, u32[]{:S(2)}, u32[]{:S(2)}) collective-permute-start(bf16[384,128]{1,0:T(8,128)(2,1)S(1)} %get-tuple-element.28), channel_id=1, source_target_pairs={{16,0},{17,1},{18,2},{19,3},{20,4},{21,5},{22,6},{23,7},{24,8},{25... | collective-permute-start | bytes 294920 | tf_op jit(solution)/shard_map/ppermute | solution.py:395
  12.7 3.7 %collective-permute-start.5 = (bf16[16,128]{1,0:T(8,128)(2,1)S(1)}, bf16[16,128]{1,0:T(8,128)(2,1)S(1)}, u32[]{:S(2)}, u32[]{:S(2)}) collective-permute-start(bf16[16,128]{1,0:T(8,128)(2,1)S(1)} %get-tuple-element.29), channel_id=1, source_target_pairs={{16,1},{17,2},{18,3},{19,4},{20,5},{21,6},{22,7},{23,8},{24,9},{25... | collective-permute-start | bytes 12296 | tf_op jit(solution)/shard_map/ppermute | solution.py:395
  16.5 0.3 fusion
  16.8 0.5 maximum_bitcast_fusion
  17.3 0.0 collective-permute-done.2.c1
  17.3 1.3 %collective-permute-start.6 = (bf16[16,128]{1,0:T(8,128)(2,1)S(1)}, bf16[16,128]{1,0:T(8,128)(2,1)S(1)}, u32[]{:S(2)}, u32[]{:S(2)}) collective-permute-start(bf16[16,128]{1,0:T(8,128)(2,1)S(1)} %get-tuple-element.30), channel_id=1, source_target_pairs={{17,0},{18,1},{19,2},{20,3},{21,4},{22,5},{23,6},{24,7},{25,8},{26... | collective-permute-start | bytes 12296 | tf_op jit(solution)/shard_map/ppermute | solution.py:395
  18.6 0.9 fusion.9
  19.5 1.6 %rev.3 = bf16[3,3,3,40,32]{3,4,2,1,0:T(8,128)(2,1)} reverse(bf16[3,3,3,40,32]{3,4,2,1,0:T(8,128)(2,1)} %param.6), dimensions={0,1,2} | reverse | bytes 138240 | tf_op jit(solution)/shard_map/rev | solution.py:462
  21.1 0.0 collective-permute-done.r1
  21.1 4.3 %shard_map.76 = (bf16[26,64,768]{2,1,0:T(8,128)(2,1)S(1)}, f32[4,80,512]{2,1,0:T(8,128)S(1)}, f32[4,176,512]{2,1,0:T(8,128)S(1)}, f32[4,176,512]{2,1,0:T(8,128)S(1)}, bf16[12,80,128]{2,1,0:T(8,128)(2,1)}) custom-call(bf16[4,64,320]{2,1,0:T(8,128)(2,1)S(1)} %copy-done.7, bf16[4,64,320]{2,1,0:T(8,128)(2,1)S(1)} %copy-done.8, ...), custom_call_target="tpu_custom_call" | custom-call | tf_op jit(solution)/shard_map/pallas_call | solution.py:361
  25.5 1.1 %copy-done.3 = f32[4,176,512]{2,1,0:T(8,128)} copy-done((f32[4,176,512]{2,1,0:T(8,128)}, f32[4,176,512]{2,1,0:T(8,128)S(1)}, u32[]{:S(2)}) %copy-start.3) | copy-done | bytes 1441816
  26.6 1.1 %copy-done.5 = f32[4,176,512]{2,1,0:T(8,128)} copy-done((f32[4,176,512]{2,1,0:T(8,128)}, f32[4,176,512]{2,1,0:T(8,128)S(1)}, u32[]{:S(2)}) %copy-start.5) | copy-done | bytes 1441816
  27.7 0.8 copy-done.9
  28.5 0.0 copy-start.12
  28.5 1.0 copy-done.12
  29.5 3.9 %shard_map.78 = (bf16[3,120,128]{2,1,0:T(8,128)(2,1)S(1)}, bf16[26,64,768]{2,1,0:T(8,128)(2,1)S(1)}) custom-call(bf16[26,64,768]{2,1,0:T(8,128)(2,1)S(1)} %get-tuple-element.25.vsh, bf16[24,64,128]{2,1,0:T(8,128)(2,1)S(1)} %copy-done.12, bf16[288,320]{1,0:T(8,128)(2,1)S(1)} %collective-permute-done.r1, bf16[32,320]{1,0:T(8,128)(2,1)S(1)} %collective-permute-done.2.c1, ...), custom_call_target="tpu_custom_call" | custom-call | tf_op jit(solution)/shard_map/pallas_call | solution.py:361
  33.4 2.5 %collective-permute-start.7 = (bf16[3,120,128]{2,1,0:T(8,128)(2,1)S(1)}, bf16[3,120,128]{2,1,0:T(8,128)(2,1)S(1)}, u32[]{:S(2)}, u32[]{:S(2)}) collective-permute-start(bf16[3,120,128]{2,1,0:T(8,128)(2,1)S(1)} %get-tuple-element.31), channel_id=1, source_target_pairs={{0,1},{1,0},{2,3},{3,2},{4,5},{5,4},{6,7},{7,6},{8,9},{9,8},{10,11... | collective-permute-start | bytes 276488 | tf_op jit(solution)/shard_map/ppermute | solution.py:506
  36.0 0.3 fusion.4
  36.3 0.6 collective-permute-done.7
  37.0 3.0 %collective-permute-start.8 = (bf16[3,120,128]{2,1,0:T(8,128)(2,1)S(1)}, bf16[3,120,128]{2,1,0:T(8,128)(2,1)S(1)}, u32[]{:S(2)}, u32[]{:S(2)}) collective-permute-start(bf16[3,120,128]{2,1,0:T(8,128)(2,1)S(1)} %add_convert_fusion.3), channel_id=1, source_target_pairs={{0,2},{1,3},{2,0},{3,1},{4,6},{5,7},{6,4},{7,5},{8,10},{9,11},{10,... | collective-permute-start | bytes 276488 | tf_op jit(solution)/shard_map/ppermute | solution.py:506
  39.9 0.5 maximum_bitcast_fusion.1
  40.4 2.5 %collective-permute-done.8 = bf16[3,120,128]{2,1,0:T(8,128)(2,1)S(1)} collective-permute-done((bf16[3,120,128]{2,1,0:T(8,128)(2,1)S(1)}, bf16[3,120,128]{2,1,0:T(8,128)(2,1)S(1)}, u32[]{:S(2)}, u32[]{:S(2)}) %collective-permute-start.8) | collective-permute-done | bytes 92192 | tf_op jit(solution)/shard_map/ppermute | solution.py:506
  42.9 0.0 copy-start.20
  43.0 3.7 %collective-permute-start.9 = (bf16[3,120,128]{2,1,0:T(8,128)(2,1)S(1)}, bf16[3,120,128]{2,1,0:T(8,128)(2,1)}, u32[]{:S(2)}, u32[]{:S(2)}) collective-permute-start(bf16[3,120,128]{2,1,0:T(8,128)(2,1)S(1)} %add_convert_fusion.2), channel_id=1, source_target_pairs={{0,4},{1,5},{2,6},{3,7},{4,0},{5,1},{6,2},{7,3},{8,12},{9,13},{10,... | collective-permute-start | bytes 276488 | tf_op jit(solution)/shard_map/ppermute | solution.py:506
  46.6 0.8 fusion.8
  47.4 1.4 %slice.59 = bf16[3,3,4,64,4,32]{3,5,1,2,0,4:T(8,128)(2,1)} slice(bf16[3,3,6,64,4,32]{3,5,1,2,0,4:T(8,128)(2,1)S(1)} %maximum_bitcast_fusion.1), slice={[0:3], [0:3], [1:5], [0:64], [0:4], [0:32]} | slice | bytes 1179648 | tf_op jit(solution)/shard_map/slice | solution.py:463
  48.7 0.1 slice-done
  48.9 1.7 %copy.14 = bf16[3,3,4,64,4,32]{3,2,1,5,4,0:T(4,128)(2,1)} copy(bf16[3,3,4,64,4,32]{3,5,1,2,0,4:T(8,128)(2,1)S(1)} %slice-done) | data formatting | bytes 1179648 | tf_op jit(solution)/shard_map/slice | solution.py:459
  50.5 2.9 %reshape.20 = bf16[3,768,128]{1,2,0:T(8,128)(2,1)} reshape(bf16[3,3,4,64,4,32]{3,2,1,5,4,0:T(4,128)(2,1)} %copy.14) | data formatting | bytes 1179648 | tf_op jit(solution)/shard_map/reshape | solution.py:459
  53.5 1.4 %copy.16.wc = bf16[3,768,128]{2,1,0:T(8,128)(2,1)S(1)} copy(bf16[3,768,128]{1,2,0:T(8,128)(2,1)} %reshape.20) | data formatting | bytes 1179648 | tf_op jit(solution)/shard_map/reshape | solution.py:459
  54.8 1.0 add_convert_fusion.1
  55.8 2.7 %collective-permute-start.10 = (bf16[3,120,128]{2,1,0:T(8,128)(2,1)S(1)}, bf16[3,120,128]{2,1,0:T(8,128)(2,1)}, u32[]{:S(2)}, u32[]{:S(2)}) collective-permute-start(bf16[3,120,128]{2,1,0:T(8,128)(2,1)S(1)} %add_convert_fusion.1), channel_id=1, source_target_pairs={{0,8},{1,9},{2,10},{3,11},{4,12},{5,13},{6,14},{7,15},{8,0},{9,1},... | collective-permute-start | bytes 276488 | tf_op jit(solution)/shard_map/ppermute | solution.py:506
  58.5 1.8 %maximum_bitcast_fusion.2 = bf16[3,3,6,32,4,64]{5,3,1,2,0,4:T(8,128)(2,1)S(1)} fusion(bf16[3,3,1,64,4,32]{3,5,1,2,0,4:T(8,128)(2,1)} %get-tuple-element.49, bf16[3,3,1,64,4,32]{3,5,1,2,0,4:T(8,128)(2,1)S(1)} %get-tuple-element.48, bf16[3,3,4,64,4,32]{3,5,1,2,0,4:T(8,128)(2,1)} %slice.59), kind=kLoop, calls=%fused_computation.2 | loop fusion | flops 884736 | bytes 1769472 | tf_op jit(solution)/shard_map/transpose | solution.py:464
  60.2 3.0 %copy.18 = bf16[3,3,6,32,4,64]{5,4,3,2,1,0:T(4,128)(2,1)} copy(bf16[3,3,6,32,4,64]{5,3,1,2,0,4:T(8,128)(2,1)S(1)} %maximum_bitcast_fusion.2) | data formatting | bytes 1769472 | tf_op jit(solution)/shard_map/transpose | solution.py:464
  63.3 3.9 %reshape.22 = bf16[3,3,192,256]{3,2,1,0:T(8,128)(2,1)} reshape(bf16[3,3,6,32,4,64]{5,4,3,2,1,0:T(4,128)(2,1)} %copy.18) | data formatting | bytes 1769472 | tf_op jit(solution)/shard_map/reshape | solution.py:464
  67.1 1.4 %pad.13 = bf16[3,3,256,256]{3,2,1,0:T(8,128)(2,1)S(1)} pad(bf16[3,3,192,256]{3,2,1,0:T(8,128)(2,1)} %reshape.22, bf16[]{:T(256)} %constant.2.clone.1), padding=0_0x0_0x0_64x0_0 | pad | bytes 2064386 | tf_op jit(solution)/shard_map/jit(_pad)/pad | solution.py:465
  68.5 0.6 collective-permute-start.3
  69.1 1.7 %copy-done.2 = bf16[26,64,768]{2,1,0:T(8,128)(2,1)S(1)} copy-done((bf16[26,64,768]{2,1,0:T(8,128)(2,1)S(1)}, bf16[26,64,768]{2,1,0:T(8,128)(2,1)}, u32[]{:S(2)}) %copy-start.2) | copy-done | bytes 2555928
  70.9 1.4 %copy-done.6 = f32[4,176,512]{2,1,0:T(8,128)S(1)} copy-done((f32[4,176,512]{2,1,0:T(8,128)S(1)}, f32[4,176,512]{2,1,0:T(8,128)}, u32[]{:S(2)}) %copy-start.6) | copy-done | bytes 1441816
  72.2 1.1 %copy-done.10 = f32[4,80,512]{2,1,0:T(8,128)S(1)} copy-done((f32[4,80,512]{2,1,0:T(8,128)S(1)}, f32[4,80,512]{2,1,0:T(8,128)}, u32[]{:S(2)}) %copy-start.10) | copy-done | bytes 655384
  73.3 7.4 %shard_map.80 = (bf16[4,64,320]{2,1,0:T(8,128)(2,1)}, bf16[4,64,320]{2,1,0:T(8,128)(2,1)S(1)}, bf16[4,64,320]{2,1,0:T(8,128)(2,1)}, bf16[4,32,320]{2,1,0:T(8,128)(2,1)}) custom-call(bf16[26,64,768]{2,1,0:T(8,128)(2,1)S(1)} %copy-done.2, bf16[3,768,256]{2,1,0:T(8,128)(2,1)S(1)} %bitcast.27, f32[4,80,512]{2,1,0:T(8,128)S(1)} %copy-done.10, ...), custom_call_target="tpu_custom_call" | custom-call | tf_op jit(solution)/shard_map/pallas_call | solution.py:361
  80.7 0.7 copy-done.13
  81.4 1.3 %collective-permute-start.12 = (bf16[4,64,320]{2,1,0:T(8,128)(2,1)}, bf16[4,64,320]{2,1,0:T(8,128)(2,1)}, u32[]{:S(2)}, u32[]{:S(2)}) collective-permute-start(bf16[4,64,320]{2,1,0:T(8,128)(2,1)} %get-tuple-element.38), channel_id=1, source_target_pairs={{1,0},{2,1},{3,2},{4,3},{5,4},{6,5},{7,6},{8,7},{9,8},{10,9},{11,1... | collective-permute-start | bytes 491528 | tf_op jit(solution)/shard_map/ppermute | solution.py:374
  82.7 1.5 %collective-permute-start.13 = (bf16[4,32,320]{2,1,0:T(8,128)(2,1)}, bf16[4,32,320]{2,1,0:T(8,128)(2,1)}, u32[]{:S(2)}, u32[]{:S(2)}) collective-permute-start(bf16[4,32,320]{2,1,0:T(8,128)(2,1)} %get-tuple-element.39), channel_id=1, source_target_pairs={{2,0},{3,1},{4,2},{5,3},{6,4},{7,5},{8,6},{9,7},{10,8},{11,9},{12,... | collective-permute-start | bytes 245768 | tf_op jit(solution)/shard_map/ppermute | solution.py:374
  84.2 0.9 add_convert_fusion.one
  85.1 1.6 %collective-permute-start.11 = (bf16[3,120,128]{2,1,0:T(8,128)(2,1)S(1)}, bf16[3,120,128]{2,1,0:T(8,128)(2,1)}, u32[]{:S(2)}, u32[]{:S(2)}) collective-permute-start(bf16[3,120,128]{2,1,0:T(8,128)(2,1)S(1)} %add_convert_fusion.one), channel_id=1, source_target_pairs={{0,16},{16,0},{1,17},{17,1},{2,18},{18,2},{3,19},{19,3},{4,20},{20... | collective-permute-start | bytes 276488 | tf_op jit(solution)/shard_map/ppermute | solution.py:506
  86.6 0.1 pad_maximum_fusion
  86.8 1.3 %copy.15 = bf16[3,3,2,64,4,32]{3,2,1,5,4,0:T(2,128)(2,1)} copy(bf16[3,3,2,64,4,32]{3,5,1,2,0,4:T(8,128)(2,1)S(1)} %pad_maximum_fusion) | data formatting | bytes 589824 | tf_op jit(solution)/shard_map/concatenate | solution.py:460
  88.1 2.2 %reshape.21 = bf16[3,384,128]{1,2,0:T(8,128)(2,1)} reshape(bf16[3,3,2,64,4,32]{3,2,1,5,4,0:T(2,128)(2,1)} %copy.15) | data formatting | bytes 589824 | tf_op jit(solution)/shard_map/reshape | solution.py:461
  90.3 1.2 %copy.17.wh = bf16[3,384,128]{2,1,0:T(8,128)(2,1)S(1)} copy(bf16[3,384,128]{1,2,0:T(8,128)(2,1)} %reshape.21) | data formatting | bytes 589824 | tf_op jit(solution)/shard_map/reshape | solution.py:461
  91.5 0.9 copy-done.14
  92.4 1.7 %shard_map.81 = bf16[4,64,320]{2,1,0:T(8,128)(2,1)} custom-call(bf16[4,64,320]{2,1,0:T(8,128)(2,1)S(1)} %copy-done.14, bf16[4,64,320]{2,1,0:T(8,128)(2,1)} %collective-permute-done.12.near, bf16[4,32,320]{2,1,0:T(8,128)(2,1)} %collective-permute-done.13.far), custom_call_target="tpu_custom_call" | custom-call | tf_op jit(solution)/shard_map/pallas_call | solution.py:361
  94.1 6.7 %shard_map.77 = bf16[24,4,64,32]{3,2,1,0:T(8,128)(2,1)S(1)} custom-call(bf16[26,64,768]{2,1,0:T(8,128)(2,1)S(1)} %get-tuple-element.25.vsh, bf16[12,80,128]{2,1,0:T(8,128)(2,1)} %collective-permute-done.3.top.bot, bf16[12,80,128]{2,1,0:T(8,128)(2,1)} %collective-permute-done.3.top.bot, bf16[3,768,128]{2,1,0:T(8,128)(2,1)S(1)} %copy.16.wc, ...), custom_call_target="tpu_custom_call" | custom-call | tf_op jit(solution)/shard_map/pallas_call | solution.py:361
  100.8 1.2 %copy-done = bf16[24,4,64,32]{3,2,1,0:T(8,128)(2,1)} copy-done((bf16[24,4,64,32]{3,2,1,0:T(8,128)(2,1)}, bf16[24,4,64,32]{3,2,1,0:T(8,128)(2,1)S(1)}, u32[]{:S(2)}) %copy-start) | copy-done | bytes 393240
  102.0 2.4 %copy.19 = bf16[24,4,64,32]{2,3,1,0:T(8,128)(2,1)} copy(bf16[24,4,64,32]{3,2,1,0:T(8,128)(2,1)} %copy-done) | data formatting | bytes 786432
  104.4 1.0 shard_map.79
  105.4 1.0 copy.20
  (41 shorter events, 0.1 us)
Async XLA Ops:
  0.6 1.9 %copy-start.7 = (bf16[4,64,320]{2,1,0:T(8,128)(2,1)S(1)}, bf16[4,64,320]{2,1,0:T(8,128)(2,1)}, u32[]{:S(2)}) copy-start(bf16[4,64,320]{2,1,0:T(8,128)(2,1)} %left.3) | copy-start | bytes 491524
  0.6 1.9 %copy-start.8 = (bf16[4,64,320]{2,1,0:T(8,128)(2,1)S(1)}, bf16[4,64,320]{2,1,0:T(8,128)(2,1)}, u32[]{:S(2)}) copy-start(bf16[4,64,320]{2,1,0:T(8,128)(2,1)} %right.3) | copy-start | bytes 491524
  0.7 15.8 %copy-start.18 = (bf16[3,3,3,40,32]{3,4,2,1,0:T(8,128)(2,1)S(1)}, bf16[3,3,3,40,32]{3,4,2,1,0:T(8,128)(2,1)}, u32[]{:S(2)}) copy-start(bf16[3,3,3,40,32]{3,4,2,1,0:T(8,128)(2,1)} %param.6) | copy-start | bytes 207364
  3.0 14.2 %copy-start.11 = (bf16[24,64,128]{2,1,0:T(8,128)(2,1)}, bf16[24,64,128]{2,1,0:T(8,128)(2,1)S(1)}, u32[]{:S(2)}) copy-start(bf16[24,64,128]{2,1,0:T(8,128)(2,1)S(1)} %get-tuple-element.27.ctl) | copy-start | bytes 1179652
  3.1 18.1 %collective-permute-start = (bf16[288,320]{1,0:T(8,128)(2,1)S(1)}, bf16[288,320]{1,0:T(8,128)(2,1)S(1)}, u32[]{:S(2)}, u32[]{:S(2)}) collective-permute-start(bf16[288,320]{1,0:T(8,128)(2,1)S(1)} %get-tuple-element.22), channel_id=1, source_target_pairs={{0,1},{1,2},{2,3},{3,4},{4,5},{5,6},{6,7},{7,8},{8,9},{9,10},{10,1... | collective-permute-start | bytes 552968 | tf_op jit(solution)/shard_map/ppermute | solution.py:374
  5.4 15.7 %collective-permute-start.1 = (bf16[128,320]{1,0:T(8,128)(2,1)S(1)}, bf16[128,320]{1,0:T(8,128)(2,1)S(1)}, u32[]{:S(2)}, u32[]{:S(2)}) collective-permute-start(bf16[128,320]{1,0:T(8,128)(2,1)S(1)} %get-tuple-element.23), channel_id=1, source_target_pairs={{0,2},{1,3},{2,4},{3,5},{4,6},{5,7},{6,8},{7,9},{8,10},{9,11},{10,... | collective-permute-start | bytes 245768 | tf_op jit(solution)/shard_map/ppermute | solution.py:374
  9.9 7.4 %collective-permute-start.2 = (bf16[32,320]{1,0:T(8,128)(2,1)S(1)}, bf16[32,320]{1,0:T(8,128)(2,1)S(1)}, u32[]{:S(2)}, u32[]{:S(2)}) collective-permute-start(bf16[32,320]{1,0:T(8,128)(2,1)S(1)} %get-tuple-element.24), channel_id=1, source_target_pairs={{1,0},{2,1},{3,2},{4,3},{5,4},{6,5},{7,6},{8,7},{9,8},{10,9},{11,1... | collective-permute-start | bytes 61448 | tf_op jit(solution)/shard_map/ppermute | solution.py:374
  11.2 17.4 %collective-permute-start.4 = (bf16[384,128]{1,0:T(8,128)(2,1)S(1)}, bf16[384,128]{1,0:T(8,128)(2,1)S(1)}, u32[]{:S(2)}, u32[]{:S(2)}) collective-permute-start(bf16[384,128]{1,0:T(8,128)(2,1)S(1)} %get-tuple-element.28), channel_id=1, source_target_pairs={{16,0},{17,1},{18,2},{19,3},{20,4},{21,5},{22,6},{23,7},{24,8},{25... | collective-permute-start | bytes 294920 | tf_op jit(solution)/shard_map/ppermute | solution.py:395
  12.7 15.8 %collective-permute-start.5 = (bf16[16,128]{1,0:T(8,128)(2,1)S(1)}, bf16[16,128]{1,0:T(8,128)(2,1)S(1)}, u32[]{:S(2)}, u32[]{:S(2)}) collective-permute-start(bf16[16,128]{1,0:T(8,128)(2,1)S(1)} %get-tuple-element.29), channel_id=1, source_target_pairs={{16,1},{17,2},{18,3},{19,4},{20,5},{21,6},{22,7},{23,8},{24,9},{25... | collective-permute-start | bytes 12296 | tf_op jit(solution)/shard_map/ppermute | solution.py:395
  17.2 3.9 %copy-start.15 = (bf16[3,3,6,64,4,32]{3,5,1,2,0,4:T(8,128)(2,1)}, bf16[3,3,6,64,4,32]{3,5,1,2,0,4:T(8,128)(2,1)S(1)}, u32[]{:S(2)}) copy-start(bf16[3,3,6,64,4,32]{3,5,1,2,0,4:T(8,128)(2,1)S(1)} %maximum_bitcast_fusion) | copy-start | bytes 2654212
  17.3 11.3 %collective-permute-start.6 = (bf16[16,128]{1,0:T(8,128)(2,1)S(1)}, bf16[16,128]{1,0:T(8,128)(2,1)S(1)}, u32[]{:S(2)}, u32[]{:S(2)}) collective-permute-start(bf16[16,128]{1,0:T(8,128)(2,1)S(1)} %get-tuple-element.30), channel_id=1, source_target_pairs={{17,0},{18,1},{19,2},{20,3},{21,4},{22,5},{23,6},{24,7},{25,8},{26... | collective-permute-start | bytes 12296 | tf_op jit(solution)/shard_map/ppermute | solution.py:395
  21.1 14.9 %copy-start.19 = (bf16[3,3,3,40,32]{3,4,2,1,0:T(8,128)(2,1)S(1)}, bf16[3,3,3,40,32]{3,4,2,1,0:T(8,128)(2,1)}, u32[]{:S(2)}) copy-start(bf16[3,3,3,40,32]{3,4,2,1,0:T(8,128)(2,1)} %rev.3) | copy-start | bytes 207364
  25.5 1.1 %copy-start.3 = (f32[4,176,512]{2,1,0:T(8,128)}, f32[4,176,512]{2,1,0:T(8,128)S(1)}, u32[]{:S(2)}) copy-start(f32[4,176,512]{2,1,0:T(8,128)S(1)} %get-tuple-element.34.fr) | copy-start | bytes 4325380
  26.5 1.1 %copy-start.5 = (f32[4,176,512]{2,1,0:T(8,128)}, f32[4,176,512]{2,1,0:T(8,128)S(1)}, u32[]{:S(2)}) copy-start(f32[4,176,512]{2,1,0:T(8,128)S(1)} %get-tuple-element.35.fr4) | copy-start | bytes 4325380
  27.7 0.8 copy-start.9
  28.5 1.0 copy-start.12
  33.4 7.0 %copy-start.1 = (bf16[26,64,768]{2,1,0:T(8,128)(2,1)}, bf16[26,64,768]{2,1,0:T(8,128)(2,1)S(1)}, u32[]{:S(2)}) copy-start(bf16[26,64,768]{2,1,0:T(8,128)(2,1)S(1)} %get-tuple-element.32.ctsh) | copy-start | bytes 7667716
  33.4 3.5 %collective-permute-start.7 = (bf16[3,120,128]{2,1,0:T(8,128)(2,1)S(1)}, bf16[3,120,128]{2,1,0:T(8,128)(2,1)S(1)}, u32[]{:S(2)}, u32[]{:S(2)}) collective-permute-start(bf16[3,120,128]{2,1,0:T(8,128)(2,1)S(1)} %get-tuple-element.31), channel_id=1, source_target_pairs={{0,1},{1,0},{2,3},{3,2},{4,5},{5,4},{6,7},{7,6},{8,9},{9,8},{10,11... | collective-permute-start | bytes 276488 | tf_op jit(solution)/shard_map/ppermute | solution.py:506
  37.0 5.9 %collective-permute-start.8 = (bf16[3,120,128]{2,1,0:T(8,128)(2,1)S(1)}, bf16[3,120,128]{2,1,0:T(8,128)(2,1)S(1)}, u32[]{:S(2)}, u32[]{:S(2)}) collective-permute-start(bf16[3,120,128]{2,1,0:T(8,128)(2,1)S(1)} %add_convert_fusion.3), channel_id=1, source_target_pairs={{0,2},{1,3},{2,0},{3,1},{4,6},{5,7},{6,4},{7,5},{8,10},{9,11},{10,... | collective-permute-start | bytes 276488 | tf_op jit(solution)/shard_map/ppermute | solution.py:506
  42.9 4.4 %copy-start.20 = (bf16[3,120,128]{2,1,0:T(8,128)(2,1)}, bf16[3,120,128]{2,1,0:T(8,128)(2,1)S(1)}, u32[]{:S(2)}) copy-start(bf16[3,120,128]{2,1,0:T(8,128)(2,1)S(1)} %add_convert_fusion.2) | copy-start | bytes 276484
  43.0 11.9 %collective-permute-start.9 = (bf16[3,120,128]{2,1,0:T(8,128)(2,1)S(1)}, bf16[3,120,128]{2,1,0:T(8,128)(2,1)}, u32[]{:S(2)}, u32[]{:S(2)}) collective-permute-start(bf16[3,120,128]{2,1,0:T(8,128)(2,1)S(1)} %add_convert_fusion.2), channel_id=1, source_target_pairs={{0,4},{1,5},{2,6},{3,7},{4,0},{5,1},{6,2},{7,3},{8,12},{9,13},{10,... | collective-permute-start | bytes 276488 | tf_op jit(solution)/shard_map/ppermute | solution.py:506
  47.4 1.5 %slice-start = ((bf16[3,3,6,64,4,32]{3,5,1,2,0,4:T(8,128)(2,1)}), bf16[3,3,4,64,4,32]{3,5,1,2,0,4:T(8,128)(2,1)S(1)}, s32[]{:S(2)}) async-start(bf16[3,3,6,64,4,32]{3,5,1,2,0,4:T(8,128)(2,1)} %copy-done.15), calls=%async_computation | async-start | bytes 2359296 | tf_op jit(solution)/shard_map/slice | solution.py:459
  55.8 28.3 %collective-permute-start.10 = (bf16[3,120,128]{2,1,0:T(8,128)(2,1)S(1)}, bf16[3,120,128]{2,1,0:T(8,128)(2,1)}, u32[]{:S(2)}, u32[]{:S(2)}) collective-permute-start(bf16[3,120,128]{2,1,0:T(8,128)(2,1)S(1)} %add_convert_fusion.1), channel_id=1, source_target_pairs={{0,8},{1,9},{2,10},{3,11},{4,12},{5,13},{6,14},{7,15},{8,0},{9,1},... | collective-permute-start | bytes 276488 | tf_op jit(solution)/shard_map/ppermute | solution.py:506
  67.1 2.0 %copy-start.4 = (f32[4,176,512]{2,1,0:T(8,128)S(1)}, f32[4,176,512]{2,1,0:T(8,128)}, u32[]{:S(2)}) copy-start(f32[4,176,512]{2,1,0:T(8,128)} %copy-done.3) | copy-start | bytes 4325380
  68.5 25.6 %collective-permute-start.3 = (bf16[12,80,128]{2,1,0:T(8,128)(2,1)}, bf16[12,80,128]{2,1,0:T(8,128)(2,1)}, u32[]{:S(2)}, u32[]{:S(2)}) collective-permute-start(bf16[12,80,128]{2,1,0:T(8,128)(2,1)} %get-tuple-element.26), channel_id=1, source_target_pairs={{16,0},{17,1},{18,2},{19,3},{20,4},{21,5},{22,6},{23,7},{24,8},{25... | collective-permute-start | bytes 737288 | tf_op jit(solution)/shard_map/ppermute | solution.py:395
  69.1 1.7 %copy-start.2 = (bf16[26,64,768]{2,1,0:T(8,128)(2,1)S(1)}, bf16[26,64,768]{2,1,0:T(8,128)(2,1)}, u32[]{:S(2)}) copy-start(bf16[26,64,768]{2,1,0:T(8,128)(2,1)} %copy-done.1) | copy-start | bytes 7667716
  70.9 1.4 %copy-start.6 = (f32[4,176,512]{2,1,0:T(8,128)S(1)}, f32[4,176,512]{2,1,0:T(8,128)}, u32[]{:S(2)}) copy-start(f32[4,176,512]{2,1,0:T(8,128)} %copy-done.5) | copy-start | bytes 4325380
  72.2 1.1 %copy-start.10 = (f32[4,80,512]{2,1,0:T(8,128)S(1)}, f32[4,80,512]{2,1,0:T(8,128)}, u32[]{:S(2)}) copy-start(f32[4,80,512]{2,1,0:T(8,128)} %copy-done.9) | copy-start | bytes 1966084
  73.3 13.3 %copy-start.16 = (bf16[3,3,1,64,4,32]{3,5,1,2,0,4:T(8,128)(2,1)S(1)}, bf16[3,3,1,64,4,32]{3,5,1,2,0,4:T(8,128)(2,1)}, u32[]{:S(2)}) copy-start(bf16[3,3,1,64,4,32]{3,5,1,2,0,4:T(8,128)(2,1)} %get-tuple-element.50) | copy-start | bytes 442372
  73.3 13.3 %copy-start.17 = (bf16[3,3,1,64,4,32]{3,5,1,2,0,4:T(8,128)(2,1)S(1)}, bf16[3,3,1,64,4,32]{3,5,1,2,0,4:T(8,128)(2,1)}, u32[]{:S(2)}) copy-start(bf16[3,3,1,64,4,32]{3,5,1,2,0,4:T(8,128)(2,1)} %get-tuple-element.51) | copy-start | bytes 442372
  80.7 0.7 copy-start.13
  81.4 10.1 %collective-permute-start.12 = (bf16[4,64,320]{2,1,0:T(8,128)(2,1)}, bf16[4,64,320]{2,1,0:T(8,128)(2,1)}, u32[]{:S(2)}, u32[]{:S(2)}) collective-permute-start(bf16[4,64,320]{2,1,0:T(8,128)(2,1)} %get-tuple-element.38), channel_id=1, source_target_pairs={{1,0},{2,1},{3,2},{4,3},{5,4},{6,5},{7,6},{8,7},{9,8},{10,9},{11,1... | collective-permute-start | bytes 491528 | tf_op jit(solution)/shard_map/ppermute | solution.py:374
  82.7 8.8 %collective-permute-start.13 = (bf16[4,32,320]{2,1,0:T(8,128)(2,1)}, bf16[4,32,320]{2,1,0:T(8,128)(2,1)}, u32[]{:S(2)}, u32[]{:S(2)}) collective-permute-start(bf16[4,32,320]{2,1,0:T(8,128)(2,1)} %get-tuple-element.39), channel_id=1, source_target_pairs={{2,0},{3,1},{4,2},{5,3},{6,4},{7,5},{8,6},{9,7},{10,8},{11,9},{12,... | collective-permute-start | bytes 245768 | tf_op jit(solution)/shard_map/ppermute | solution.py:374
  85.1 19.3 %collective-permute-start.11 = (bf16[3,120,128]{2,1,0:T(8,128)(2,1)S(1)}, bf16[3,120,128]{2,1,0:T(8,128)(2,1)}, u32[]{:S(2)}, u32[]{:S(2)}) collective-permute-start(bf16[3,120,128]{2,1,0:T(8,128)(2,1)S(1)} %add_convert_fusion.one), channel_id=1, source_target_pairs={{0,16},{16,0},{1,17},{17,1},{2,18},{18,2},{3,19},{19,3},{4,20},{20... | collective-permute-start | bytes 276488 | tf_op jit(solution)/shard_map/ppermute | solution.py:506
  91.5 0.9 copy-start.14
  100.8 1.2 %copy-start = (bf16[24,4,64,32]{3,2,1,0:T(8,128)(2,1)}, bf16[24,4,64,32]{3,2,1,0:T(8,128)(2,1)S(1)}, u32[]{:S(2)}) copy-start(bf16[24,4,64,32]{3,2,1,0:T(8,128)(2,1)S(1)} %shard_map.77) | copy-start | bytes 1179652

commit v2 on v1

--- a/solution.py
+++ b/solution.py
@@ -15,7 +15,7 @@
 F32 = jnp.float32
 BF16 = jnp.bfloat16
 VMEM = pl.BlockSpec(memory_space=pltpu.VMEM)
-LIMIT = 40 * 1024 * 1024
+LIMIT = 16 * 1024 * 1024
 
 
 def params():
@@ -26,28 +26,32 @@
     return lax.broadcasted_iota(jnp.int32, shape, len(shape) - 1)
 
 
-def channel_table(channels, group_size, flip):
+def channel_table(channels, group_size, flip, value=1.0):
     shape = (group_size * SLOT, channels) if flip else (channels, group_size * SLOT)
     c = lax.broadcasted_iota(jnp.int32, shape, 1 if flip else 0)
     j = lax.broadcasted_iota(jnp.int32, shape, 0 if flip else 1)
-    hit = (lax.rem(c, group_size) == lax.div(j, SLOT)) & (lax.div(c, group_size) == lax.rem(j, SLOT))
-    return jnp.where(hit, 1.0, 0.0).astype(BF16)
+    hit = c == (j & (SLOT - 1)) * group_size + (j >> (SLOT.bit_length() - 1))
+    return jnp.where(hit, value, 0.0).astype(BF16)
 
 
 def dot(a, b):
     return jnp.dot(a, b, preferred_element_type=F32)
+
+
+def dot_nt(a, b):
+    return lax.dot_general(a, b, (((1,), (1,)), ((), ())), preferred_element_type=F32)
 
 
 def pack_kernel(ends, left, right, ct, r1, r2, c1, ctl, *rest):
     n = len(ends)
     row_refs, lo_refs, hi_refs = rest[:n], rest[n : 2 * n], rest[2 * n : 3 * n]
     ctf, rowf = rest[3 * n :]
-    disp, rows, cols, feat = ct.shape
+    disp, rows, feat, cols = ct.shape
     for h in range(rows):
         r1[h * cols : (h + 1) * cols] = right[h]
         r2[h * (cols // 2) : (h + 1) * (cols // 2)] = right[h, cols // 2 :]
     for d in range(disp):
-        block = jnp.concatenate([ct[d, h].astype(F32) for h in range(rows)], axis=1)
+        block = ct[d].reshape(rows * feat, cols).astype(F32).T
         ctf[d * cols : (d + 1) * cols] = block
         ctl[d] = block.astype(BF16)
     width = rows * feat
@@ -62,8 +66,8 @@
         h = end()
         for q in range(disp // per):
             rowf[q * cols : (q + 1) * cols] = jnp.concatenate(
-                [ct[q * per + i, h].astype(F32) for i in range(per)], axis=1
-            )
+                [ct[q * per + i, h].astype(F32) for i in range(per)], axis=0
+            ).T
         row_ref[...] = rowf[...].astype(BF16)
         for ref, col in ((lo_ref, 0), (hi_ref, cols - 1)):
             ref[...] = jnp.zeros(ref.shape, BF16)
@@ -82,19 +86,21 @@
         return dot(x, table)
 
     base = rows * cols
-    edge_l = spread(r1[base : base + 32])
     edge_r = spread(c1[...])
     far = spread(r2[...])
     near = spread(r1[0:base])
     own = spread(right[...].reshape(base, channels))
-    own_l = spread(left[...].reshape(base, channels))
+    scaled = channel_table(channels, group_size, False, 1.0 / group_size)
+    own_l = dot(left[...].reshape(base, channels), scaled)
+    edge_ll = dot(r1[base : base + 32], scaled)
+    edge_lr = dot(c1[...], scaled)
     half = cols // 2
     for h in range(rows):
         fl[h, 0:PAD] = jnp.zeros((PAD, wide), F32)
         fl[h, PAD + cols :] = jnp.zeros((PAD, wide), F32)
-        fl[h, PAD - 1 : PAD] = edge_l[disp + h : disp + h + 1]
+        fl[h, PAD - 1 : PAD] = edge_ll[disp + h : disp + h + 1]
         fl[h, PAD : PAD + cols] = own_l[h * cols : (h + 1) * cols]
-        fl[h, PAD + cols : PAD + cols + 1] = edge_r[disp + h : disp + h + 1]
+        fl[h, PAD + cols : PAD + cols + 1] = edge_lr[disp + h : disp + h + 1]
         for ref, off in ((fr, 0), (fr4, STEP)):
             start = reach - cols - half + off
             ref[h, 0:start] = jnp.zeros((start, wide), F32)
@@ -111,49 +117,57 @@
     total = cols + 2 * PAD
     block = 16
     low = lanes((block, 128)) < SLOT
-    scale = 1.0 / group_size
-
-    def pair(dd, _):
+    pairs = rows // 2
+
+    def products(i, _):
+        p, b = lax.rem(i, pairs), lax.div(i, pairs)
+        at = pl.multiple_of(b * block, block)
+        lefts = [fl[2 * p + o, pl.ds(at, block)] for o in range(2)]
+        for d in range(disp):
+            band = fr4 if d % 2 else fr
+            start = pl.multiple_of(at + reach - PAD - 2 * STEP * (d // 2), 8)
+            sums = []
+            for o in range(2):
+                prod = lefts[o] * band[2 * p + o, pl.ds(start, block)]
+                acc = prod[:, 0:128]
+                for j in range(1, wide // 128):
+                    acc = acc + prod[:, 128 * j : 128 * (j + 1)]
+                sums.append(acc + pltpu.roll(acc, SLOT, 1))
+            vbuf[p, d, pl.ds(at, block)] = jnp.where(low, sums[0], sums[1])
+        return 0
+
+    lax.fori_loop(0, pairs * (total // block), products, 0)
+    big = lanes((total, 128)) < SLOT
+
+    def spread_taps(dd, _):
         for odd in range(2):
-            band = fr4 if odd else fr
-            for b in range(total // block):
-                at = pl.multiple_of(reach - PAD + b * block - 2 * STEP * dd, 8)
-                sums = []
-                for h in range(rows):
-                    prod = fl[h, b * block : (b + 1) * block] * band[h, pl.ds(at, block)]
-                    acc = prod[:, 0:128]
-                    for j in range(1, wide // 128):
-                        acc = acc + prod[:, 128 * j : 128 * (j + 1)]
-                    sums.append((acc + pltpu.roll(acc, SLOT, 1)) * scale)
-                for p in range(rows // 2):
-                    vbuf[odd, b * block : (b + 1) * block, 128 * p : 128 * (p + 1)] = jnp.where(
-                        low, sums[2 * p], sums[2 * p + 1]
-                    )
-            for e in range(3):
-                vsh[2 * dd + odd + 1, :, 256 * e : 256 * (e + 1)] = vbuf[
-                    odd, PAD - 1 + e : PAD - 1 + e + cols
-                ].astype(BF16)
-        big = lanes((total, 128)) < SLOT
+            d = 2 * dd + odd
+            for p in range(pairs):
+                for e in range(3):
+                    lane = 128 * (pairs * e + p)
+                    vsh[d + 1, :, lane : lane + 128] = vbuf[
+                        p, d, PAD - 1 + e : PAD - 1 + e + cols
+                    ].astype(BF16)
         for end, pay in zip(ends, pays):
             h = end()
             if isinstance(h, int):
-                lane = 128 * (h // 2)
-                halves = [vbuf[o, :, lane : lane + 128] for o in range(2)]
+                halves = [vbuf[h // 2, 2 * dd + o] for o in range(2)]
                 if h % 2 == 0:
                     halves[1] = pltpu.roll(halves[1], SLOT, 1)
                 else:
                     halves[0] = pltpu.roll(halves[0], SLOT, 1)
                 out = jnp.where(big, halves[0], halves[1])
             else:
-                first = jnp.where(big, vbuf[0, :, 0:128], pltpu.roll(vbuf[1, :, 0:128], SLOT, 1))
-                last = jnp.where(
-                    big, pltpu.roll(vbuf[0, :, 128:256], SLOT, 1), vbuf[1, :, 128:256]
+                last = pairs - 1
+                first = jnp.where(big, vbuf[0, 2 * dd], pltpu.roll(vbuf[0, 2 * dd + 1], SLOT, 1))
+                final = jnp.where(
+                    big, pltpu.roll(vbuf[last, 2 * dd], SLOT, 1), vbuf[last, 2 * dd + 1]
                 )
-                out = jnp.where(h == 0, first, last)
+                out = jnp.where(h == 0, first, final)
             pay[dd] = out.astype(BF16)
         return 0
 
-    lax.fori_loop(0, disp // 2, pair, 0)
+    lax.fori_loop(0, disp // 2, spread_taps, 0)
 
 
 def weight_kernel(
@@ -227,17 +241,13 @@
     lax.fori_loop(0, 3, taps, 0)
 
 
-def feature_kernel(group_size, ctsh, w2, fl, fr, fr4, lg, rg0, rg1, rg2, gv, accl, accr):
+def feature_kernel(group_size, ctsh, w2, fl, fr, fr4, lg, rg0, rg1, rg2, gv, accl, acce, acco):
     disp = ctsh.shape[0] - 2
     rows, cols, channels = lg.shape
     reach = fr.shape[1] - cols - PAD
     wide = group_size * SLOT
     step = 256 // cols
     low = lanes((256, 128)) < SLOT
-    scale = 1.0 / group_size
-    for h in range(rows):
-        gv[h, :, 0:PAD] = jnp.zeros((disp, PAD, 128), F32)
-        gv[h, :, PAD + cols :] = jnp.zeros((disp, PAD, 128), F32)
 
     def conv(q, _):
         acc = None
@@ -245,46 +255,53 @@
             block = ctsh[pl.ds(q * step + a, step)].reshape(256, ctsh.shape[2])
             part = dot(block, w2[a])
             acc = part if acc is None else acc + part
-        g = acc.astype(BF16).astype(F32) * scale
+        g = acc.astype(BF16).astype(F32)
         for p in range(rows // 2):
             x = g[:, 128 * p : 128 * (p + 1)]
             r = pltpu.roll(x, SLOT, 1)
             for o in range(2):
                 y = jnp.where(low, r, x) if o else jnp.where(low, x, r)
-                gv[2 * p + o, pl.ds(q * step, step), PAD : PAD + cols] = y.reshape(step, cols, 128)
+                gv[2 * p + o, pl.ds(q * step, step)] = y.reshape(step, cols, 128)
         return 0
 
     lax.fori_loop(0, disp // step, conv, 0)
+    block = 16
 
     def left_block(i, _):
-        h = lax.div(i, cols // 8)
-        w = pl.multiple_of(lax.rem(i, cols // 8) * 8, 8)
-        accs = [jnp.zeros((8, 128), F32) for _ in range(wide // 128)]
+        h = lax.div(i, cols // block)
+        w = pl.multiple_of(lax.rem(i, cols // block) * block, block)
+        accs = [jnp.zeros((block, 128), F32) for _ in range(wide // 128)]
         for d in range(disp):
             band = fr4 if d % 2 else fr
             at = pl.multiple_of(w + reach - 2 * STEP * (d // 2), 8)
-            g = gv[h, d, pl.ds(w + PAD, 8)]
+            g = gv[h, d, pl.ds(w, block)]
             for j in range(wide // 128):
-                accs[j] = accs[j] + g * band[h, pl.ds(at, 8), 128 * j : 128 * (j + 1)]
+                accs[j] = accs[j] + g * band[h, pl.ds(at, block), 128 * j : 128 * (j + 1)]
         for j in range(wide // 128):
-            accl[h, pl.ds(w, 8), 128 * j : 128 * (j + 1)] = accs[j]
-        return 0
-
-    lax.fori_loop(0, rows * (cols // 8), left_block, 0)
-    back = accr.shape[1] - cols
+            accl[h, pl.ds(w, block), 128 * j : 128 * (j + 1)] = accs[j] * (1.0 / group_size)
+        return 0
+
+    lax.fori_loop(0, rows * (cols // block), left_block, 0)
+    count = cols // 8
+    back = acce.shape[1] - cols
+    lead = back // 8
 
     def right_row(h, _):
-        for u in range(-back, cols, 8):
-            accs = [jnp.zeros((8, 128), F32) for _ in range(wide // 128)]
-            for d in range(disp):
-                w = u + STEP * d
-                if w <= -8 or w >= cols:
-                    continue
-                g = gv[h, d, w + PAD : w + PAD + 8]
+        for odd, buf in enumerate((acce, acco)):
+            for k in range(lead + count):
+                accs = [jnp.zeros((8, 128), F32) for _ in range(wide // 128)]
+                for t in range(disp // 2):
+                    b = k + t - lead
+                    if b < 0 or b >= count:
+                        continue
+                    g = gv[h, 2 * t + odd, 8 * b : 8 * b + 8]
+                    for j in range(wide // 128):
+                        accs[j] = accs[j] + g * fl[
+                            h, PAD + 8 * b : PAD + 8 * b + 8, 128 * j : 128 * (j + 1)
+                        ]
                 for j in range(wide // 128):
-                    accs[j] = accs[j] + g * fl[h, w + PAD : w + PAD + 8, 128 * j : 128 * (j + 1)]
-            for j in range(wide // 128):
-                accr[h, u + back : u + back + 8, 128 * j : 128 * (j + 1)] = accs[j]
+                    buf[h, 8 * k : 8 * k + 8, 128 * j : 128 * (j + 1)] = accs[j]
+        acco[h, 8 * (lead + count) :] = jnp.zeros((8, wide), F32)
         return 0
 
     lax.fori_loop(0, rows, right_row, 0)
@@ -292,14 +309,15 @@
     half = cols // 2
     for h in range(rows):
         lg[h] = dot(accl[h].astype(BF16), table).astype(BF16)
-        whole = dot(accr[h].astype(BF16), table).astype(BF16)
+        both = acce[h] + acco[h, STEP : STEP + back + cols]
+        whole = dot(both.astype(BF16), table).astype(BF16)
         rg2[h] = whole[back - cols - half : back - cols]
         rg1[h] = whole[back - cols : back]
         rg0[h] = whole[back:]
 
 
 def conv_kernel(masks, vsh, top, bot, wc, wh, out, halo, buf):
-    disp, rows, cols, feat = out.shape
+    disp, rows, feat, cols = out.shape
     mtop, mbot = masks()
     total = top.shape[1]
     low = lanes((total, 128)) < SLOT
@@ -326,35 +344,80 @@
         for a in range(3):
             main = vsh[pl.ds(q * step + a, step)].reshape(256, vsh.shape[2])
             side = halo[pl.ds(q * step + a, step)].reshape(256, halo.shape[2])
-            part = dot(main, wc[a]) + dot(side, wh[a])
+            part = dot_nt(wc[a], main) + dot_nt(wh[a], side)
             acc = part if acc is None else acc + part
+        acc = acc.astype(BF16)
         for i in range(step):
-            for h in range(rows):
-                out[q * step + i, h] = acc[
-                    i * cols : (i + 1) * cols, feat * h : feat * (h + 1)
-                ].astype(BF16)
+            out[q * step + i] = acc[:, i * cols : (i + 1) * cols].reshape(rows, feat, cols)
         return 0
 
     lax.fori_loop(0, disp // step, conv, 0)
 
 
-def finish_weight_kernel(scale, one, two, out):
-    _, _, _, groups, feat = out.shape
+def finish_kernel(scale, count, *refs):
+    parts, (own, near, far, weight, right) = refs[:count], refs[count:]
+    _, _, _, feat, groups = weight.shape
     for a in range(3):
+        total = tree([ref[a].astype(F32) for ref in parts]) * scale
         for e in range(3):
-            at = groups * e
-            x = (one[a, at : at + groups].astype(F32) + two[a, at : at + groups].astype(F32)) * scale
+            x = total[groups * e : groups * (e + 1)].T
             for b in range(3):
-                out[2 - a, 2 - b, 2 - e] = x[:, feat * b : feat * (b + 1)]
-
-
-def finish_right_kernel(own, near, far, out):
-    rows, cols, channels = out.shape
+                weight[2 - a, 2 - b, 2 - e] = x[feat * b : feat * (b + 1)]
+    rows, cols, channels = right.shape
     half = cols // 2
     for h in range(rows):
         total = own[h].astype(F32) + near[h].astype(F32)
-        out[h, 0:half] = total[0:half].astype(BF16)
-        out[h, half:] = (total[half:] + far[h].astype(F32)).astype(BF16)
+        right[h, 0:half] = total[0:half].astype(BF16)
+        right[h, half:] = (total[half:] + far[h].astype(F32)).astype(BF16)
+
+
+def tree(terms):
+    while len(terms) > 1:
+        terms = [terms[i] + terms[i + 1] for i in range(0, len(terms), 2)]
+    return terms[0]
+
+
+def taps_kernel(taps, w2, wc, wh):
+    _, _, _, feat, groups = taps.shape
+    rows = wc.shape[1] // feat
+    low = lanes((feat, 2 * SLOT)) < SLOT
+    zero = jnp.zeros((feat, 2 * SLOT), F32)
+
+    def wide(a, b, e):
+        if not 0 <= b <= 2:
+            return None
+        return jnp.concatenate([taps[a, b, e].astype(F32), zero[:, groups:]], axis=1)
+
+    def beside(x, y):
+        if x is None and y is None:
+            return zero.astype(BF16)
+        x = zero if x is None else x
+        y = zero if y is None else pltpu.roll(y, SLOT, 1)
+        return jnp.where(low, x, y).astype(BF16)
+
+    def build(a, _):
+        for e in range(3):
+            for h in range(rows):
+                for p in range(rows // 2):
+                    lane = SLOT * (rows * e + 2 * p)
+                    wc[a, feat * h : feat * (h + 1), lane : lane + 2 * SLOT] = beside(
+                        wide(a, 2 * p - h + 1, e), wide(a, 2 * p + 1 - h + 1, e)
+                    )
+                wh[a, feat * h : feat * (h + 1), 2 * SLOT * e : 2 * SLOT * (e + 1)] = beside(
+                    wide(a, 0, e) if h == 0 else None, wide(a, 2, e) if h == rows - 1 else None
+                )
+            for slot, six in enumerate((*range(1, rows + 1), 0, rows + 1)):
+                at = 256 * e + feat * slot
+                for p in range(rows // 2):
+                    back = [2 - (six - 2 * p - o) for o in range(2)]
+                    w2[a, at : at + feat, 2 * SLOT * p : 2 * SLOT * (p + 1)] = beside(
+                        wide(2 - a, back[0], 2 - e), wide(2 - a, back[1], 2 - e)
+                    )
+            at = 256 * e + feat * (rows + 2)
+            w2[a, at : 256 * (e + 1)] = jnp.zeros((256 - feat * (rows + 2), rows * SLOT), BF16)
+        return 0
+
+    lax.fori_loop(0, 3, build, 0)
 
 
 def call(kernel, outs, scratch, *args):
@@ -402,11 +465,16 @@
     return grid_shift(pays[0], 1, distance), grid_shift(pays[1], -1, distance)
 
 
-def banded(conv_weight, rows):
-    _, _, _, groups, _ = conv_weight.shape
-    padded = jnp.pad(conv_weight, ((0, 0), (rows - 1, rows - 1), (0, 0), (0, SLOT - groups), (0, 0)))
-    stack = [padded[:, rows - 1 - h : 2 * rows + 1 - h] for h in range(rows)]
-    return jnp.stack(stack, axis=4).transpose(0, 2, 1, 3, 4, 5)
+def stages(n_row, n_col):
+    col_bits = [1 << i for i in range(n_col.bit_length() - 1)]
+    row_bits = [n_col << i for i in range(n_row.bit_length() - 1)]
+    assert n_col == 1 << len(col_bits) and n_row == 1 << len(row_bits)
+    rest = col_bits[1:2] + row_bits + col_bits[2:]
+    out = [col_bits[:1]]
+    for i in range(0, len(rest), 2):
+        pair = rest[i : i + 2]
+        out.append(pair + [sum(pair)] if len(pair) == 2 else pair)
+    return out
 
 
 def on_device(left_features, right_features, conv_weight, cotangent):
@@ -444,7 +512,7 @@
         [pltpu.VMEM((disp * cols, rows * feat), F32), pltpu.VMEM((disp // per * cols, 128), F32)],
         left_features,
         right_features,
-        cotangent,
+        cotangent.transpose(0, 1, 3, 2),
     )
     r1, r2, c1, ctl = packed[:4]
     row_pay, lo_pay, hi_pay = packed[4 : 4 + n], packed[4 + n : 4 + 2 * n], packed[4 + 2 * n :]
@@ -455,15 +523,16 @@
     tl, bl = halos(hi_pay, 1)
     tr, br = halos(lo_pay, -1)
 
-    six = banded(conv_weight, rows)
-    wc = six[:, :, 1 : rows + 1].reshape(3, 3 * rows * SLOT, rows * feat)
-    wh = jnp.concatenate([six[:, :, :1], six[:, :, rows + 1 :]], axis=2)
-    wh = wh.reshape(3, 3 * 2 * SLOT, rows * feat)
-    back = banded(conv_weight[::-1, ::-1, ::-1], rows)
-    back = jnp.concatenate([back[:, :, 1 : rows + 1], back[:, :, :1], back[:, :, rows + 1 :]], axis=2)
-    back = back.transpose(0, 1, 2, 5, 4, 3).reshape(3, 3, (rows + 2) * feat, rows * SLOT)
-    w2 = jnp.pad(back, ((0, 0), (0, 0), (0, 256 - (rows + 2) * feat), (0, 0)))
-    w2 = w2.reshape(3, 3 * 256, rows * SLOT)
+    w2, wc, wh = call(
+        taps_kernel,
+        [
+            ((3, 3 * 256, rows * SLOT), BF16),
+            ((3, rows * feat, 3 * rows * SLOT), BF16),
+            ((3, rows * feat, 3 * 2 * SLOT), BF16),
+        ],
+        [],
+        conv_weight.transpose(0, 1, 2, 4, 3),
+    )
 
     band = 104 + cols + PAD
     volume = call(
@@ -475,7 +544,7 @@
             ((rows, band, wide), F32),
         ]
         + [((disp // 2, cols + 2 * PAD, 128), BF16)] * n,
-        [pltpu.VMEM((2, cols + 2 * PAD, rows * SLOT), F32)],
+        [pltpu.VMEM((rows // 2, disp, cols + 2 * PAD, 2 * SLOT), F32)],
         left_features,
         right_features,
         r1,
@@ -496,16 +565,14 @@
         vsh, ctl, r1, c1, top, bot, tl, bl, tr, br,
     )
 
-    hops = []
-    for axis, size in (("col", n_col), ("row", n_row)):
-        bit = 1
-        while bit < size:
-            hops.append((axis, [(i, i ^ bit) for i in range(size)]))
-            bit *= 2
-    for step, (axis, route) in enumerate(hops):
-        other = lax.ppermute(part, axis, route)
-        if step < len(hops) - 1:
-            part = (part.astype(F32) + other.astype(F32)).astype(BF16)
+    parts = None
+    for masks_of in stages(n_row, n_col):
+        if parts is not None:
+            part = tree([x.astype(F32) for x in parts]).astype(BF16)
+        parts = [part] + [
+            lax.ppermute(part, ("row", "col"), [(i, i ^ m) for i in range(n_row * n_col)])
+            for m in masks_of
+        ]
     cells = disp * rows * n_row * cols * n_col
 
     lg, rg0, rg1, rg2 = call(
@@ -517,9 +584,10 @@
             ((rows, cols // 2, channels), BF16),
         ],
         [
-            pltpu.VMEM((rows, disp, cols + 2 * PAD, 128), F32),
+            pltpu.VMEM((rows, disp, cols, 128), F32),
             pltpu.VMEM((rows, cols, wide), F32),
             pltpu.VMEM((rows, cols + cols + cols // 2, wide), F32),
+            pltpu.VMEM((rows, cols + cols + cols // 2 + 8, wide), F32),
         ],
         ctsh, w2, fl, fr, fr4,
     )
@@ -528,24 +596,25 @@
 
     (output,) = call(
         functools.partial(conv_kernel, masks),
-        [((disp, rows, cols, feat), BF16)],
+        [((disp, rows, feat, cols), BF16)],
         [
             pltpu.VMEM((disp + 2, cols, 3 * 2 * SLOT), BF16),
             pltpu.VMEM((2, cols + 2 * PAD, 128), F32),
         ],
         vsh, vtop, vbot, wc, wh,
     )
-    (right_grad,) = call(
-        finish_right_kernel, [((rows, cols, channels), BF16)], [], rg0, rg1, rg2
-    )
-    (weight_grad,) = call(
-        functools.partial(finish_weight_kernel, 1.0 / math.sqrt(cells)),
-        [(conv_weight.shape, F32)],
+    weight_grad, right_grad = call(
+        functools.partial(finish_kernel, 1.0 / math.sqrt(cells), len(parts)),
+        [((3, 3, 3, feat, groups), F32), ((rows, cols, channels), BF16)],
         [],
-        part,
-        other,
-    )
-    return (output, weight_grad, lg, right_grad)
+        *parts, rg0, rg1, rg2,
+    )
+    return (
+        output.transpose(0, 1, 3, 2),
+        weight_grad.transpose(0, 1, 2, 4, 3),
+        lg,
+        right_grad,
+    )
 
 
 def solution(mesh):

time: 108 us -> 63.1 us (0.58); the launches traced: 106 us -> 62.8 us
  local copies, waits for them, and re-layouts: 40.6 us -> 2.98 us
  other arithmetic: 4.74 us -> 0.08 us
  Pallas kernels: 25.6 us -> 23.2 us
  waiting for transfers between devices: 3.17 us -> 4.51 us
    unnamed x45 -> x8, local copies, waits for them, and re-layouts: 16.3 us -> 2.98 us
    reshape x5 -> x0, local copies, waits for them, and re-layouts: 11.6 us -> none  [the longest x2 4.29 us: on_device(): wc = six[:, :, 1:rows + 1].reshape(3, 3 * rows * SLOT, rows * feat)]
    slice x6 -> x0, local copies, waits for them, and re-layouts: 4.82 us -> none  [the longest x3 1.81 us: on_device(): wc = six[:, :, 1:rows + 1].reshape(3, 3 * rows * SLOT, rows * feat)]
    transpose x1 -> x0, local copies, waits for them, and re-layouts: 3.04 us -> none  [on_device(): back.transpose(0, 1, 2, 5, 4, 3)]
    transpose x3 -> x0, other arithmetic: 2.68 us -> none  [the longest x1 1.76 us: on_device(): back.transpose(0, 1, 2, 5, 4, 3)]
    pallas_call x7, Pallas kernels: 25.6 us -> 23.2 us  [call(): pl.pallas_call(kernel, out_shape=[jax.ShapeDtypeStruct(s, t) for s, t in...]
    convert_element_type x4 -> x2, other arithmetic: 1.94 us -> 0.08 us  [on_device(): part = tree([x.astype(F32) for x in parts]).astype(BF16)]
    ppermute x4, starting transfers between devices: 7.17 us -> 8.86 us  [grid_swap(): return lax.ppermute(block, ('row', 'col'), route)]
  transfers between devices with their start and end apart: 14 -> 16, of which waited for: 2 -> 3; matrix products, arithmetic and copies ran while one was open for 28% -> 0% of each run, Pallas kernels for 19% -> 29%
where the time goes in v2:
time: 63.1 us; the launch traced here: 62.8 us
  starting transfers between devices  31.2 us (49%)
  Pallas kernels  23.2 us (37%)
  waiting for transfers between devices  4.51 us (7%)
  local copies, waits for them, and re-layouts  2.98 us (5%)
  between operations  0.8 us (1%)
    pallas_call x7, Pallas kernels, call(): pl.pallas_call(kernel, out_shape=[jax.ShapeDtypeStruct(s, t) for s, t in...  23.2 us
    ppermute x7, starting transfers between devices, on_device(): lax.ppermute(part, ('row', 'col'), [(i, i ^ m) for i in range(n_row * n_c...  12.5 us
    ppermute x5, starting transfers between devices, col_shift(): return lax.ppermute(block, 'col', route)  9.81 us
    ppermute x4, starting transfers between devices, grid_swap(): return lax.ppermute(block, ('row', 'col'), route)  8.86 us
    ppermute x7, waiting for transfers between devices, on_device(): lax.ppermute(part, ('row', 'col'), [(i, i ^ m) for i in range(n_row * n_c...  3.86 us
    unnamed x8, local copies, waits for them, and re-layouts  2.98 us
  transfers between devices with their start and end apart: 16, of which 3 were waited for; matrix products, arithmetic and copies ran while one was open for 0% of the time, Pallas kernels for 29%

profile of v2, /device:TPU:0, one launch (start us, length us, event | category | flops | bytes accessed | tf_op | source)
XLA Modules:
  0.0 62.8 jit_solution(4738932760485463837)
XLA Ops:
  0.6 0.0 copy-start
  0.6 1.1 %copy-done = bf16[24,4,64,32]{2,3,1,0:T(8,128)(2,1)S(1)} copy-done((bf16[24,4,64,32]{2,3,1,0:T(8,128)(2,1)S(1)}, bf16[24,4,64,32]{2,3,1,0:T(8,128)(2,1)}, u32[]{:S(2)}) %copy-start) | copy-done | bytes 393240
  1.8 0.0 copy-start.1
  1.8 0.9 %copy-done.1 = bf16[4,64,320]{2,1,0:T(8,128)(2,1)S(1)} copy-done((bf16[4,64,320]{2,1,0:T(8,128)(2,1)S(1)}, bf16[4,64,320]{2,1,0:T(8,128)(2,1)}, u32[]{:S(2)}) %copy-start.1) | copy-done | bytes 163864
  2.7 0.0 copy-start.2
  2.7 0.9 %copy-done.2 = bf16[4,64,320]{2,1,0:T(8,128)(2,1)S(1)} copy-done((bf16[4,64,320]{2,1,0:T(8,128)(2,1)S(1)}, bf16[4,64,320]{2,1,0:T(8,128)(2,1)}, u32[]{:S(2)}) %copy-start.2) | copy-done | bytes 163864
  3.6 0.4 shard_map.75
  4.0 2.4 %collective-permute-start = (bf16[288,320]{1,0:T(8,128)(2,1)S(1)}, bf16[288,320]{1,0:T(8,128)(2,1)S(1)}, u32[]{:S(2)}, u32[]{:S(2)}) collective-permute-start(bf16[288,320]{1,0:T(8,128)(2,1)S(1)} %get-tuple-element.27), channel_id=1, source_target_pairs={{0,1},{1,2},{2,3},{3,4},{4,5},{5,6},{6,7},{7,8},{8,9},{9,10},{10,1... | collective-permute-start | bytes 552968 | tf_op jit(solution)/shard_map/ppermute | solution.py:437
  6.4 2.4 %collective-permute-start.4 = (bf16[384,128]{1,0:T(8,128)(2,1)S(1)}, bf16[384,128]{1,0:T(8,128)(2,1)S(1)}, u32[]{:S(2)}, u32[]{:S(2)}) collective-permute-start(bf16[384,128]{1,0:T(8,128)(2,1)S(1)} %get-tuple-element.35), channel_id=1, source_target_pairs={{16,0},{17,1},{18,2},{19,3},{20,4},{21,5},{22,6},{23,7},{24,8},{25... | collective-permute-start | bytes 294920 | tf_op jit(solution)/shard_map/ppermute | solution.py:458
  8.7 3.6 %collective-permute-start.1 = (bf16[128,320]{1,0:T(8,128)(2,1)S(1)}, bf16[128,320]{1,0:T(8,128)(2,1)S(1)}, u32[]{:S(2)}, u32[]{:S(2)}) collective-permute-start(bf16[128,320]{1,0:T(8,128)(2,1)S(1)} %get-tuple-element.28), channel_id=1, source_target_pairs={{0,2},{1,3},{2,4},{3,5},{4,6},{5,7},{6,8},{7,9},{8,10},{9,11},{10,... | collective-permute-start | bytes 245768 | tf_op jit(solution)/shard_map/ppermute | solution.py:437
  12.3 1.3 %collective-permute-start.2 = (bf16[32,320]{1,0:T(8,128)(2,1)S(1)}, bf16[32,320]{1,0:T(8,128)(2,1)S(1)}, u32[]{:S(2)}, u32[]{:S(2)}) collective-permute-start(bf16[32,320]{1,0:T(8,128)(2,1)S(1)} %get-tuple-element.29), channel_id=1, source_target_pairs={{1,0},{2,1},{3,2},{4,3},{5,4},{6,5},{7,6},{8,7},{9,8},{10,9},{11,1... | collective-permute-start | bytes 61448 | tf_op jit(solution)/shard_map/ppermute | solution.py:437
  13.6 3.7 %collective-permute-start.5 = (bf16[16,128]{1,0:T(8,128)(2,1)S(1)}, bf16[16,128]{1,0:T(8,128)(2,1)S(1)}, u32[]{:S(2)}, u32[]{:S(2)}) collective-permute-start(bf16[16,128]{1,0:T(8,128)(2,1)S(1)} %get-tuple-element.36), channel_id=1, source_target_pairs={{16,1},{17,2},{18,3},{19,4},{20,5},{21,6},{22,7},{23,8},{24,9},{25... | collective-permute-start | bytes 12296 | tf_op jit(solution)/shard_map/ppermute | solution.py:458
  17.4 0.0 collective-permute-done.2.c1
  17.4 1.3 %collective-permute-start.6 = (bf16[16,128]{1,0:T(8,128)(2,1)S(1)}, bf16[16,128]{1,0:T(8,128)(2,1)S(1)}, u32[]{:S(2)}, u32[]{:S(2)}) collective-permute-start(bf16[16,128]{1,0:T(8,128)(2,1)S(1)} %get-tuple-element.37), channel_id=1, source_target_pairs={{17,0},{18,1},{19,2},{20,3},{21,4},{22,5},{23,6},{24,7},{25,8},{26... | collective-permute-start | bytes 12296 | tf_op jit(solution)/shard_map/ppermute | solution.py:458
  18.7 0.0 collective-permute-done.1.r2
  18.7 0.0 collective-permute-done.r1
  18.7 3.9 %shard_map.76 = (bf16[26,64,768]{2,1,0:T(8,128)(2,1)S(1)}, f32[4,80,512]{2,1,0:T(8,128)S(1)}, f32[4,176,512]{2,1,0:T(8,128)S(1)}, f32[4,176,512]{2,1,0:T(8,128)S(1)}, bf16[12,80,128]{2,1,0:T(8,128)(2,1)S(1)}) custom-call(bf16[4,64,320]{2,1,0:T(8,128)(2,1)S(1)} %copy-done.1, bf16[4,64,320]{2,1,0:T(8,128)(2,1)S(1)} %copy-done.2, ...), custom_call_target="tpu_custom_call" | custom-call | tf_op jit(solution)/shard_map/pallas_call | solution.py:424
  22.6 0.0 collective-permute-done.5.tl.bl
  22.6 0.6 %collective-permute-done.6.tr.br = bf16[16,128]{1,0:T(8,128)(2,1)S(1)} collective-permute-done((bf16[16,128]{1,0:T(8,128)(2,1)S(1)}, bf16[16,128]{1,0:T(8,128)(2,1)S(1)}, u32[]{:S(2)}, u32[]{:S(2)}) %collective-permute-start.6) | collective-permute-done | bytes 4128 | tf_op jit(solution)/shard_map/ppermute | solution.py:458
  23.2 0.0 collective-permute-done.4.top.bot
  23.2 0.0 copy-start.3
  23.2 3.9 %shard_map.79 = (bf16[3,120,128]{2,1,0:T(8,128)(2,1)S(1)}, bf16[26,64,768]{2,1,0:T(8,128)(2,1)S(1)}) custom-call(bf16[26,64,768]{2,1,0:T(8,128)(2,1)S(1)} %get-tuple-element.30.vsh, bf16[24,64,128]{2,1,0:T(8,128)(2,1)S(1)} %get-tuple-element.34.ctl, bf16[288,320]{1,0:T(8,128)(2,1)S(1)} %collective-permute-done.r1, ...), custom_call_target="tpu_custom_call" | custom-call | tf_op jit(solution)/shard_map/pallas_call | solution.py:424
  27.2 1.7 %collective-permute-start.7 = (bf16[3,120,128]{2,1,0:T(8,128)(2,1)S(1)}, bf16[3,120,128]{2,1,0:T(8,128)(2,1)S(1)}, u32[]{:S(2)}, u32[]{:S(2)}) collective-permute-start(bf16[3,120,128]{2,1,0:T(8,128)(2,1)S(1)} %get-tuple-element.38), channel_id=1, source_target_pairs={{0,1},{1,0},{2,3},{3,2},{4,5},{5,4},{6,7},{7,6},{8,9},{9,8},{10,11... | collective-permute-start | bytes 276488 | tf_op jit(solution)/shard_map/ppermute | solution.py:573
  28.8 0.9 %collective-permute-done.7 = bf16[3,120,128]{2,1,0:T(8,128)(2,1)S(1)} collective-permute-done((bf16[3,120,128]{2,1,0:T(8,128)(2,1)S(1)}, bf16[3,120,128]{2,1,0:T(8,128)(2,1)S(1)}, u32[]{:S(2)}, u32[]{:S(2)}) %collective-permute-start.7) | collective-permute-done | bytes 92192 | tf_op jit(solution)/shard_map/ppermute | solution.py:573
  29.8 4.2 %collective-permute-start.10 = (bf16[3,120,128]{2,1,0:T(8,128)(2,1)S(1)}, bf16[3,120,128]{2,1,0:T(8,128)(2,1)S(1)}, u32[]{:S(2)}, u32[]{:S(2)}) collective-permute-start(bf16[3,120,128]{2,1,0:T(8,128)(2,1)S(1)} %add_convert_fusion.1), channel_id=1, source_target_pairs={{0,18},{1,19},{2,16},{3,17},{4,22},{5,23},{6,20},{7,21},{8,26},{9,... | collective-permute-start | bytes 276488 | tf_op jit(solution)/shard_map/ppermute | solution.py:573
  34.1 0.5 collective-permute-start.9
  34.6 0.1 collective-permute-start.8
  34.7 0.0 copy-done.3
  34.7 0.5 shard_map.77
  35.2 1.5 %collective-permute-start.3 = (bf16[12,80,128]{2,1,0:T(8,128)(2,1)S(1)}, bf16[12,80,128]{2,1,0:T(8,128)(2,1)S(1)}, u32[]{:S(2)}, u32[]{:S(2)}) collective-permute-start(bf16[12,80,128]{2,1,0:T(8,128)(2,1)S(1)} %get-tuple-element.31), channel_id=1, source_target_pairs={{16,0},{17,1},{18,2},{19,3},{20,4},{21,5},{22,6},{23,7},{24,8},{25... | collective-permute-start | bytes 737288 | tf_op jit(solution)/shard_map/ppermute | solution.py:458
  36.6 7.1 %shard_map.80 = (bf16[4,64,320]{2,1,0:T(8,128)(2,1)}, bf16[4,64,320]{2,1,0:T(8,128)(2,1)S(1)}, bf16[4,64,320]{2,1,0:T(8,128)(2,1)S(1)}, bf16[4,32,320]{2,1,0:T(8,128)(2,1)S(1)}) custom-call(bf16[26,64,768]{2,1,0:T(8,128)(2,1)S(1)} %get-tuple-element.39.ctsh, bf16[3,768,256]{2,1,0:T(8,128)(2,1)S(1)} %get-tuple-element.40.w2, ...), custom_call_target="tpu_custom_call" | custom-call | tf_op jit(solution)/shard_map/pallas_call | solution.py:424
  43.7 1.3 %collective-permute-start.14 = (bf16[4,64,320]{2,1,0:T(8,128)(2,1)S(1)}, bf16[4,64,320]{2,1,0:T(8,128)(2,1)S(1)}, u32[]{:S(2)}, u32[]{:S(2)}) collective-permute-start(bf16[4,64,320]{2,1,0:T(8,128)(2,1)S(1)} %get-tuple-element.45), channel_id=1, source_target_pairs={{1,0},{2,1},{3,2},{4,3},{5,4},{6,5},{7,6},{8,7},{9,8},{10,9},{11,1... | collective-permute-start | bytes 491528 | tf_op jit(solution)/shard_map/ppermute | solution.py:437
  45.0 0.0 collective-permute-done.10
  45.0 0.0 collective-permute-done.9
  45.0 0.0 collective-permute-done.8
  45.0 0.1 add_convert_fusion.refs_0_
  45.1 5.3 %collective-permute-start.13 = (bf16[3,120,128]{2,1,0:T(8,128)(2,1)S(1)}, bf16[3,120,128]{2,1,0:T(8,128)(2,1)S(1)}, u32[]{:S(2)}, u32[]{:S(2)}) collective-permute-start(bf16[3,120,128]{2,1,0:T(8,128)(2,1)S(1)} %add_convert_fusion.refs_0_), channel_id=1, source_target_pairs={{0,12},{1,13},{2,14},{3,15},{4,8},{5,9},{6,10},{7,11},{8,4},{9,5},... | collective-permute-start | bytes 276488 | tf_op jit(solution)/shard_map/ppermute | solution.py:573
  50.3 0.0 collective-permute-start.12
  50.3 0.6 %collective-permute-start.11 = (bf16[3,120,128]{2,1,0:T(8,128)(2,1)S(1)}, bf16[3,120,128]{2,1,0:T(8,128)(2,1)S(1)}, u32[]{:S(2)}, u32[]{:S(2)}) collective-permute-start(bf16[3,120,128]{2,1,0:T(8,128)(2,1)S(1)} %add_convert_fusion.refs_0_), channel_id=1, source_target_pairs={{0,4},{1,5},{2,6},{3,7},{4,0},{5,1},{6,2},{7,3},{8,12},{9,13},{10,... | collective-permute-start | bytes 276488 | tf_op jit(solution)/shard_map/ppermute | solution.py:573
  51.0 0.0 collective-permute-done.3.top.bot
  51.0 1.3 %collective-permute-start.15 = (bf16[4,32,320]{2,1,0:T(8,128)(2,1)S(1)}, bf16[4,32,320]{2,1,0:T(8,128)(2,1)S(1)}, u32[]{:S(2)}, u32[]{:S(2)}) collective-permute-start(bf16[4,32,320]{2,1,0:T(8,128)(2,1)S(1)} %get-tuple-element.46), channel_id=1, source_target_pairs={{2,0},{3,1},{4,2},{5,3},{6,4},{7,5},{8,6},{9,7},{10,8},{11,9},{12,... | collective-permute-start | bytes 245768 | tf_op jit(solution)/shard_map/ppermute | solution.py:437
  52.3 6.6 %shard_map.78 = bf16[24,4,32,64]{3,2,1,0:T(8,128)(2,1)} custom-call(bf16[26,64,768]{2,1,0:T(8,128)(2,1)S(1)} %get-tuple-element.30.vsh, bf16[12,80,128]{2,1,0:T(8,128)(2,1)S(1)} %collective-permute-done.3.top.bot, bf16[12,80,128]{2,1,0:T(8,128)(2,1)S(1)} %collective-permute-done.3.top.bot, bf16[3,128,768]{2,1,0:T(8,128)(2,1)S(1)} %get-tuple-element.32.wc, ...), custom_call_target="tpu_custom_call" | custom-call | tf_op jit(solution)/shard_map/pallas_call | solution.py:424
  58.8 0.0 collective-permute-done.15.refs_6_
  58.8 0.0 collective-permute-done.14.refs_5_
  58.8 0.0 collective-permute-done.13.refs_3_
  58.8 2.9 %collective-permute-done.12.refs_2_ = bf16[3,120,128]{2,1,0:T(8,128)(2,1)S(1)} collective-permute-done((bf16[3,120,128]{2,1,0:T(8,128)(2,1)S(1)}, bf16[3,120,128]{2,1,0:T(8,128)(2,1)S(1)}, u32[]{:S(2)}, u32[]{:S(2)}) %collective-permute-start.12) | collective-permute-done | bytes 92192 | tf_op jit(solution)/shard_map/ppermute | solution.py:573
  61.7 0.0 collective-permute-done.11.refs_1_
  61.7 1.0 %shard_map.81 = (f32[3,3,3,32,40]{4,3,2,1,0:T(8,128)}, bf16[4,64,320]{2,1,0:T(8,128)(2,1)}) custom-call(bf16[3,120,128]{2,1,0:T(8,128)(2,1)S(1)} %add_convert_fusion.refs_0_, bf16[3,120,128]{2,1,0:T(8,128)(2,1)S(1)} %collective-permute-done.11.refs_1_, bf16[3,120,128]{2,1,0:T(8,128)(2,1)S(1)} %collective-permute-done.12.refs_2_, ...), custom_call_target="tpu_custom_call" | custom-call | tf_op jit(solution)/shard_map/pallas_call | solution.py:424
  (1 shorter events, 0.0 us)
Async XLA Ops:
  0.6 1.1 %copy-start = (bf16[24,4,64,32]{2,3,1,0:T(8,128)(2,1)S(1)}, bf16[24,4,64,32]{2,3,1,0:T(8,128)(2,1)}, u32[]{:S(2)}) copy-start(bf16[24,4,64,32]{2,3,1,0:T(8,128)(2,1)} %param.7) | copy-start | bytes 1179652
  1.8 0.9 %copy-start.1 = (bf16[4,64,320]{2,1,0:T(8,128)(2,1)S(1)}, bf16[4,64,320]{2,1,0:T(8,128)(2,1)}, u32[]{:S(2)}) copy-start(bf16[4,64,320]{2,1,0:T(8,128)(2,1)} %left.3) | copy-start | bytes 491524
  2.7 0.9 %copy-start.2 = (bf16[4,64,320]{2,1,0:T(8,128)(2,1)S(1)}, bf16[4,64,320]{2,1,0:T(8,128)(2,1)}, u32[]{:S(2)}) copy-start(bf16[4,64,320]{2,1,0:T(8,128)(2,1)} %right.3) | copy-start | bytes 491524
  4.0 14.7 %collective-permute-start = (bf16[288,320]{1,0:T(8,128)(2,1)S(1)}, bf16[288,320]{1,0:T(8,128)(2,1)S(1)}, u32[]{:S(2)}, u32[]{:S(2)}) collective-permute-start(bf16[288,320]{1,0:T(8,128)(2,1)S(1)} %get-tuple-element.27), channel_id=1, source_target_pairs={{0,1},{1,2},{2,3},{3,4},{4,5},{5,6},{6,7},{7,8},{8,9},{9,10},{10,1... | collective-permute-start | bytes 552968 | tf_op jit(solution)/shard_map/ppermute | solution.py:437
  6.4 16.9 %collective-permute-start.4 = (bf16[384,128]{1,0:T(8,128)(2,1)S(1)}, bf16[384,128]{1,0:T(8,128)(2,1)S(1)}, u32[]{:S(2)}, u32[]{:S(2)}) collective-permute-start(bf16[384,128]{1,0:T(8,128)(2,1)S(1)} %get-tuple-element.35), channel_id=1, source_target_pairs={{16,0},{17,1},{18,2},{19,3},{20,4},{21,5},{22,6},{23,7},{24,8},{25... | collective-permute-start | bytes 294920 | tf_op jit(solution)/shard_map/ppermute | solution.py:458
  8.7 9.9 %collective-permute-start.1 = (bf16[128,320]{1,0:T(8,128)(2,1)S(1)}, bf16[128,320]{1,0:T(8,128)(2,1)S(1)}, u32[]{:S(2)}, u32[]{:S(2)}) collective-permute-start(bf16[128,320]{1,0:T(8,128)(2,1)S(1)} %get-tuple-element.28), channel_id=1, source_target_pairs={{0,2},{1,3},{2,4},{3,5},{4,6},{5,7},{6,8},{7,9},{8,10},{9,11},{10,... | collective-permute-start | bytes 245768 | tf_op jit(solution)/shard_map/ppermute | solution.py:437
  12.3 5.0 %collective-permute-start.2 = (bf16[32,320]{1,0:T(8,128)(2,1)S(1)}, bf16[32,320]{1,0:T(8,128)(2,1)S(1)}, u32[]{:S(2)}, u32[]{:S(2)}) collective-permute-start(bf16[32,320]{1,0:T(8,128)(2,1)S(1)} %get-tuple-element.29), channel_id=1, source_target_pairs={{1,0},{2,1},{3,2},{4,3},{5,4},{6,5},{7,6},{8,7},{9,8},{10,9},{11,1... | collective-permute-start | bytes 61448 | tf_op jit(solution)/shard_map/ppermute | solution.py:437
  13.6 9.0 %collective-permute-start.5 = (bf16[16,128]{1,0:T(8,128)(2,1)S(1)}, bf16[16,128]{1,0:T(8,128)(2,1)S(1)}, u32[]{:S(2)}, u32[]{:S(2)}) collective-permute-start(bf16[16,128]{1,0:T(8,128)(2,1)S(1)} %get-tuple-element.36), channel_id=1, source_target_pairs={{16,1},{17,2},{18,3},{19,4},{20,5},{21,6},{22,7},{23,8},{24,9},{25... | collective-permute-start | bytes 12296 | tf_op jit(solution)/shard_map/ppermute | solution.py:458
  17.4 5.9 %collective-permute-start.6 = (bf16[16,128]{1,0:T(8,128)(2,1)S(1)}, bf16[16,128]{1,0:T(8,128)(2,1)S(1)}, u32[]{:S(2)}, u32[]{:S(2)}) collective-permute-start(bf16[16,128]{1,0:T(8,128)(2,1)S(1)} %get-tuple-element.37), channel_id=1, source_target_pairs={{17,0},{18,1},{19,2},{20,3},{21,4},{22,5},{23,6},{24,7},{25,8},{26... | collective-permute-start | bytes 12296 | tf_op jit(solution)/shard_map/ppermute | solution.py:458
  23.2 11.5 %copy-start.3 = (bf16[3,3,3,40,32]{3,4,2,1,0:T(8,128)(2,1)S(1)}, bf16[3,3,3,40,32]{3,4,2,1,0:T(8,128)(2,1)}, u32[]{:S(2)}) copy-start(bf16[3,3,3,40,32]{3,4,2,1,0:T(8,128)(2,1)} %param.6) | copy-start | bytes 207364
  27.2 2.6 %collective-permute-start.7 = (bf16[3,120,128]{2,1,0:T(8,128)(2,1)S(1)}, bf16[3,120,128]{2,1,0:T(8,128)(2,1)S(1)}, u32[]{:S(2)}, u32[]{:S(2)}) collective-permute-start(bf16[3,120,128]{2,1,0:T(8,128)(2,1)S(1)} %get-tuple-element.38), channel_id=1, source_target_pairs={{0,1},{1,0},{2,3},{3,2},{4,5},{5,4},{6,7},{7,6},{8,9},{9,8},{10,11... | collective-permute-start | bytes 276488 | tf_op jit(solution)/shard_map/ppermute | solution.py:573
  29.8 15.2 %collective-permute-start.10 = (bf16[3,120,128]{2,1,0:T(8,128)(2,1)S(1)}, bf16[3,120,128]{2,1,0:T(8,128)(2,1)S(1)}, u32[]{:S(2)}, u32[]{:S(2)}) collective-permute-start(bf16[3,120,128]{2,1,0:T(8,128)(2,1)S(1)} %add_convert_fusion.1), channel_id=1, source_target_pairs={{0,18},{1,19},{2,16},{3,17},{4,22},{5,23},{6,20},{7,21},{8,26},{9,... | collective-permute-start | bytes 276488 | tf_op jit(solution)/shard_map/ppermute | solution.py:573
  34.1 10.9 %collective-permute-start.9 = (bf16[3,120,128]{2,1,0:T(8,128)(2,1)S(1)}, bf16[3,120,128]{2,1,0:T(8,128)(2,1)S(1)}, u32[]{:S(2)}, u32[]{:S(2)}) collective-permute-start(bf16[3,120,128]{2,1,0:T(8,128)(2,1)S(1)} %add_convert_fusion.1), channel_id=1, source_target_pairs={{0,16},{1,17},{2,18},{3,19},{4,20},{5,21},{6,22},{7,23},{8,24},{9,... | collective-permute-start | bytes 276488 | tf_op jit(solution)/shard_map/ppermute | solution.py:573
  34.6 10.4 %collective-permute-start.8 = (bf16[3,120,128]{2,1,0:T(8,128)(2,1)S(1)}, bf16[3,120,128]{2,1,0:T(8,128)(2,1)S(1)}, u32[]{:S(2)}, u32[]{:S(2)}) collective-permute-start(bf16[3,120,128]{2,1,0:T(8,128)(2,1)S(1)} %add_convert_fusion.1), channel_id=1, source_target_pairs={{0,2},{1,3},{2,0},{3,1},{4,6},{5,7},{6,4},{7,5},{8,10},{9,11},{10,... | collective-permute-start | bytes 276488 | tf_op jit(solution)/shard_map/ppermute | solution.py:573
  35.2 15.8 %collective-permute-start.3 = (bf16[12,80,128]{2,1,0:T(8,128)(2,1)S(1)}, bf16[12,80,128]{2,1,0:T(8,128)(2,1)S(1)}, u32[]{:S(2)}, u32[]{:S(2)}) collective-permute-start(bf16[12,80,128]{2,1,0:T(8,128)(2,1)S(1)} %get-tuple-element.31), channel_id=1, source_target_pairs={{16,0},{17,1},{18,2},{19,3},{20,4},{21,5},{22,6},{23,7},{24,8},{25... | collective-permute-start | bytes 737288 | tf_op jit(solution)/shard_map/ppermute | solution.py:458
  43.7 15.1 %collective-permute-start.14 = (bf16[4,64,320]{2,1,0:T(8,128)(2,1)S(1)}, bf16[4,64,320]{2,1,0:T(8,128)(2,1)S(1)}, u32[]{:S(2)}, u32[]{:S(2)}) collective-permute-start(bf16[4,64,320]{2,1,0:T(8,128)(2,1)S(1)} %get-tuple-element.45), channel_id=1, source_target_pairs={{1,0},{2,1},{3,2},{4,3},{5,4},{6,5},{7,6},{8,7},{9,8},{10,9},{11,1... | collective-permute-start | bytes 491528 | tf_op jit(solution)/shard_map/ppermute | solution.py:437
  45.1 13.8 %collective-permute-start.13 = (bf16[3,120,128]{2,1,0:T(8,128)(2,1)S(1)}, bf16[3,120,128]{2,1,0:T(8,128)(2,1)S(1)}, u32[]{:S(2)}, u32[]{:S(2)}) collective-permute-start(bf16[3,120,128]{2,1,0:T(8,128)(2,1)S(1)} %add_convert_fusion.refs_0_), channel_id=1, source_target_pairs={{0,12},{1,13},{2,14},{3,15},{4,8},{5,9},{6,10},{7,11},{8,4},{9,5},... | collective-permute-start | bytes 276488 | tf_op jit(solution)/shard_map/ppermute | solution.py:573
  50.3 11.4 %collective-permute-start.12 = (bf16[3,120,128]{2,1,0:T(8,128)(2,1)S(1)}, bf16[3,120,128]{2,1,0:T(8,128)(2,1)S(1)}, u32[]{:S(2)}, u32[]{:S(2)}) collective-permute-start(bf16[3,120,128]{2,1,0:T(8,128)(2,1)S(1)} %add_convert_fusion.refs_0_), channel_id=1, source_target_pairs={{0,8},{1,9},{2,10},{3,11},{4,12},{5,13},{6,14},{7,15},{8,0},{9,1},... | collective-permute-start | bytes 276488 | tf_op jit(solution)/shard_map/ppermute | solution.py:573
  50.3 11.4 %collective-permute-start.11 = (bf16[3,120,128]{2,1,0:T(8,128)(2,1)S(1)}, bf16[3,120,128]{2,1,0:T(8,128)(2,1)S(1)}, u32[]{:S(2)}, u32[]{:S(2)}) collective-permute-start(bf16[3,120,128]{2,1,0:T(8,128)(2,1)S(1)} %add_convert_fusion.refs_0_), channel_id=1, source_target_pairs={{0,4},{1,5},{2,6},{3,7},{4,0},{5,1},{6,2},{7,3},{8,12},{9,13},{10,... | collective-permute-start | bytes 276488 | tf_op jit(solution)/shard_map/ppermute | solution.py:573
  51.0 7.8 %collective-permute-start.15 = (bf16[4,32,320]{2,1,0:T(8,128)(2,1)S(1)}, bf16[4,32,320]{2,1,0:T(8,128)(2,1)S(1)}, u32[]{:S(2)}, u32[]{:S(2)}) collective-permute-start(bf16[4,32,320]{2,1,0:T(8,128)(2,1)S(1)} %get-tuple-element.46), channel_id=1, source_target_pairs={{2,0},{3,1},{4,2},{5,3},{6,4},{7,5},{8,6},{9,7},{10,8},{11,9},{12,... | collective-permute-start | bytes 245768 | tf_op jit(solution)/shard_map/ppermute | solution.py:437
